TPU v7x, 32 devices: a whole 2x2x4 slice. The times are simulated.
32 devices in a mesh: plane: 4 (over z), pencil: 8 (over y, x, core).
Axes of the slice: x: 2, y: 2, z: 4, core: 2. Of those that a mesh axis runs over, the one named last changes fastest.
Arguments:
- velocity: float32 [8, 5120, 3840], P('plane', 'pencil'), may hold values from -6 to 6
- plane_slot: int32 [8], replicated, may hold values from 0 to 7, as said below
- pair_list: int32 [20, 2], replicated, may hold values from 0 to 7, as said below
Outputs:
- band_cross: float32 [8, 4, 2, 1024, 512], P('plane', None, None, 'pencil')
- partner_cross: float32 [8, 4, 2, 1024, 512], P('plane', None, None, 'pencil')
Inputs may be any that keep to these rules, and one draw needn't show every extreme that they name: Plane q is held in slot plane_slot[q] of velocity; that slot lies in the same aligned block of 2 slots as q, and every slot holds exactly one plane. `pair_list`: each row (a, b) satisfies a <= b < a + 4; no row appears twice; rows (0, 0) and (7, 7) are present.
All inputs are finite; a program needn't handle non-finite values.
Results may differ from a plain program's by a relative error of at most 0.000088.
Values sent between devices are 32-bit elements; how exact they have to be, the bound alone decides.
No kernel may reach another device: no remote copies, remote signals or barrier semaphores. Data moves between devices by JAX's collectives and lax.ppermute only.
A program may use at most 128 MiB of HBM per device.

v0:
```python
import math

import jax
import jax.numpy as jnp
from jax import lax
from jax.sharding import PartitionSpec as P

NX = 5120
NZ = 3840
KX = 512
KZ = 1024


highest = lax.Precision.HIGHEST


def spanwise_table(first_col, col_block, mode_share):
    column = first_col + lax.broadcasted_iota(jnp.int32, (NZ, col_block), 1)
    span_pos = lax.broadcasted_iota(jnp.int32, (NZ, col_block), 0)
    wavenumber = column // (2 * mode_share) * mode_share + column % mode_share
    phase_angle = (wavenumber * span_pos % NZ).astype(jnp.float32) * (2.0 * math.pi / NZ)
    return jnp.where(column // mode_share % 2 == 0, jnp.cos(phase_angle), -jnp.sin(phase_angle))


def axial_table(first_row, row_block):
    axial_pos = first_row + lax.broadcasted_iota(jnp.int32, (row_block, 2 * KX), 0)
    column = lax.broadcasted_iota(jnp.int32, (row_block, 2 * KX), 1)
    wavenumber = column % KX
    wavenumber = jnp.where(wavenumber < KX // 2, wavenumber, wavenumber - KX + NX)
    phase_angle = (wavenumber * axial_pos % NX).astype(jnp.float32) * (2.0 * math.pi / NX)
    return jnp.where(column < KX, jnp.cos(phase_angle), jnp.sin(phase_angle))


def combine_parts(totals, mode_share):
    item_count = totals.shape[0]
    parted = totals.reshape(item_count, 2, mode_share, 2, KX)
    real_part = parted[:, 0, :, 0] + parted[:, 1, :, 1]
    imag_part = parted[:, 1, :, 0] - parted[:, 0, :, 1]
    return jnp.stack([real_part, imag_part], axis=1) * (1.0 / math.sqrt(NX * NZ))


def cross_product(first, second):
    real_part = (
        first[..., 0, :, :] * second[..., 0, :, :] + first[..., 1, :, :] * second[..., 1, :, :]
    )
    imag_part = (
        first[..., 1, :, :] * second[..., 0, :, :] - first[..., 0, :, :] * second[..., 1, :, :]
    )
    return jnp.stack([real_part, imag_part], axis=-3)


def local(velocity, plane_slot, pair_list):
    planes = velocity.shape[0]
    row_count = velocity.shape[1]
    mode_share = KZ // lax.axis_size("pencil")
    reach = lax.axis_size("plane") // 2
    band_span = planes * reach
    flat_field = velocity.reshape(planes * row_count, NZ)
    col_block = min(2 * KZ, 512)
    pieces = []
    for first_col in range(0, 2 * KZ, col_block):
        pieces.append(
            jnp.dot(
                flat_field,
                spanwise_table(first_col, col_block, mode_share),
                precision=highest,
                preferred_element_type=jnp.float32,
            )
        )
    halfway = jnp.concatenate(pieces, axis=1).reshape(planes, row_count, 2 * KZ)
    items = lax.all_to_all(halfway, "pencil", split_axis=2, concat_axis=1, tiled=True)
    totals = jnp.zeros((items.shape[0], 2 * mode_share, 2 * KX), jnp.float32)
    row_block = min(NX, 1280)
    for first_row in range(0, NX, row_block):
        totals = totals + jnp.einsum(
            "nxc,xk->nck",
            items[:, first_row : first_row + row_block],
            axial_table(first_row, row_block),
            precision=highest,
            preferred_element_type=jnp.float32,
        )
    spectra_slot = combine_parts(totals, mode_share)
    first_plane = lax.axis_index("plane") * planes
    held = lax.dynamic_slice_in_dim(plane_slot, first_plane, planes, 0) - first_plane
    spectra = jnp.take(spectra_slot, held, axis=0)
    lower_plane = pair_list[:, 0]
    upper_plane = pair_list[:, 1]
    pair_gap = upper_plane - lower_plane
    slot_codes = lax.broadcasted_iota(jnp.int32, (planes * band_span, 1), 0)
    wanted_up = jnp.any(
        slot_codes == ((lower_plane - first_plane) * band_span + pair_gap)[None, :], axis=1
    ).reshape(planes, band_span, 1, 1, 1)
    wanted_down = jnp.any(
        slot_codes == ((upper_plane - first_plane) * band_span + pair_gap)[None, :], axis=1
    ).reshape(planes, band_span, 1, 1, 1)
    conj_sign = jnp.array([1.0, -1.0], jnp.float32).reshape(2, 1, 1)
    own_index = lax.broadcasted_iota(jnp.int32, (planes, band_span), 0)
    gap_index = lax.broadcasted_iota(jnp.int32, (planes, band_span), 1)
    full_shape = (planes, band_span, 2, mode_share, KX)
    everything = lax.all_gather(spectra, "plane", axis=0, tiled=True)
    partners = jnp.take(
        everything, (first_plane + own_index + gap_index).reshape(-1), axis=0, mode="clip"
    ).reshape(full_shape)
    band_cross = jnp.where(wanted_up, cross_product(spectra[:, None], partners), 0.0)
    earlier = jnp.take(
        everything, (first_plane + own_index - gap_index).reshape(-1), axis=0, mode="clip"
    ).reshape(full_shape)
    partner_cross = jnp.where(
        wanted_down, cross_product(earlier, spectra[:, None]) * conj_sign, 0.0
    )
    return (band_cross, partner_cross)


def solution(mesh):
    return jax.shard_map(
        local,
        mesh=mesh,
        in_specs=(P("plane", "pencil", None), P(), P()),
        out_specs=(P("plane", None, None, "pencil", None), P("plane", None, None, "pencil", None)),
        check_vma=False,
    )
```

profile of v0, /device:TPU:0, one launch (start us, length us, event | category | flops | bytes accessed | tf_op | source)
XLA Modules:
  0.0 811.1 jit_solution(1531130911370505903)
XLA Ops:
  7.4 97.2 %fusion.181 = f32[1280,512]{0,1:T(8,128)S(1)} fusion(f32[1280,3840]{1,0:T(8,128)} %bitcast.74, s32[512]{0:T(512)S(1)} %get-tuple-element.46, s32[512]{0:T(512)S(1)} %get-tuple-element.47, s32[512]{0:T(512)S(1)} %get-tuple-element.44, s32[512]{0:T(512)S(1)} %get-tuple-element.50, s32[512]{0:T(512)S(1)} %get-tuple-element.45, s32[512]{0:T(512)S(1)} %get-tuple-element.51, ...), kind=kOutput, calls=%fused_computation.205 | convolution fusion | flops 30254039040 | bytes 22296064 | tf_op jit(solution)/shard_map/dot_general | solution.py:63
  104.6 97.5 %fusion.184 = f32[1280,512]{0,1:T(8,128)S(1)} fusion(f32[1280,3840]{1,0:T(8,128)} %bitcast.75, s32[512]{0:T(512)S(1)} %get-tuple-element.38, s32[512]{0:T(512)S(1)} %get-tuple-element.39, s32[512]{0:T(512)S(1)} %get-tuple-element.36, s32[512]{0:T(512)S(1)} %get-tuple-element.42, s32[512]{0:T(512)S(1)} %get-tuple-element.37, s32[512]{0:T(512)S(1)} %get-tuple-element.43, ...), kind=kOutput, calls=%fused_computation.206 | convolution fusion | flops 30254039040 | bytes 22296064 | tf_op jit(solution)/shard_map/dot_general | solution.py:63
  202.2 97.8 %fusion.187 = f32[1280,512]{0,1:T(8,128)S(1)} fusion(f32[1280,3840]{1,0:T(8,128)} %bitcast.76, s32[512]{0:T(512)S(1)} %get-tuple-element.30, s32[512]{0:T(512)S(1)} %get-tuple-element.31, s32[512]{0:T(512)S(1)} %get-tuple-element.28, s32[512]{0:T(512)S(1)} %get-tuple-element.34, s32[512]{0:T(512)S(1)} %get-tuple-element.29, s32[512]{0:T(512)S(1)} %get-tuple-element.35, ...), kind=kOutput, calls=%fused_computation.207 | convolution fusion | flops 30254039040 | bytes 22296064 | tf_op jit(solution)/shard_map/dot_general | solution.py:63
  300.0 97.4 %fusion.190 = f32[1280,512]{0,1:T(8,128)S(1)} fusion(f32[1280,3840]{1,0:T(8,128)} %bitcast.77, s32[512]{0:T(512)S(1)} %get-tuple-element.22, s32[512]{0:T(512)S(1)} %get-tuple-element.23, s32[512]{0:T(512)S(1)} %get-tuple-element.20, s32[512]{0:T(512)S(1)} %get-tuple-element.26, s32[512]{0:T(512)S(1)} %get-tuple-element.21, s32[512]{0:T(512)S(1)} %get-tuple-element.27, ...), kind=kOutput, calls=%fused_computation.208 | convolution fusion | flops 30254039040 | bytes 22296064 | tf_op jit(solution)/shard_map/dot_general | solution.py:63
  397.4 4.5 pad_maximum_fusion
  401.9 13.1 %reshape.161 = f32[2,640,2048]{1,0,2:T(2,128)} reshape(f32[1280,2048]{0,1:T(8,128)} %pad_maximum_fusion) | data formatting | bytes 20971520 | tf_op jit(solution)/shard_map/reshape | solution.py:70
  415.0 5.3 all-to-all-start
  420.3 0.2 all-gather.2.cloned.1.call-start
  420.7 116.8 %all-to-all-done = f32[2,640,2048]{1,0,2:T(2,128)} async-done(((f32[2,640,2048]{1,0,2:T(2,128)}), f32[2,640,2048]{1,0,2:T(2,128)}, u32[]{:S(2)}, u32[]{:S(2)}) %all-to-all-start) | async-done | bytes 10485792 | tf_op jit(solution)/shard_map/all_to_all | solution.py:71
  537.5 13.9 %copy.37 = f32[2,640,8,256]{1,2,3,0:T(8,128)} copy(f32[2,640,8,256]{1,0,3,2:T(2,128)} %bitcast.6) | data formatting | bytes 20971520 | tf_op jit(solution)/shard_map/all_to_all | solution.py:71
  551.4 12.0 %all_to_all.16 = f32[2,5120,256]{1,2,0:T(8,128)} reshape(f32[2,8,640,256]{2,1,3,0:T(8,128)} %bitcast.71) | data formatting | bytes 20971520 | tf_op jit(solution)/shard_map/all_to_all | solution.py:71
  563.4 1.9 fusion.346
  565.3 1.9 fusion.348
  567.2 1.9 fusion.344
  569.1 1.9 fusion.350
  571.0 31.0 %fusion.82 = f32[2,256,1024]{2,1,0:T(8,128)S(1)} fusion(s32[1280]{0:T(1024)S(1)} %iota_add_fusion.1, s32[1024]{0:T(1024)S(1)} %iota_and_fusion, s32[1024]{0:T(1024)S(1)} %fusion.242, pred[1024]{0:T(1024)(128)(4,1)S(1)} %get-tuple-element.53, pred[1024]{0:T(1024)(128)(4,1)S(1)} %get-tuple-element.52, f32[2,1280,256]{1,2,0:T(8,128)S(1)} %fusion.346), kind=kOutput, calls=%fused_computation.108 | convolution fusion | flops 8071413760 | bytes 4733952 | tf_op jit(solution)/shard_map/nxc,xk->nck/dot_general | solution.py:75
  602.1 31.5 %fusion.84 = f32[2,256,1024]{2,1,0:T(8,128)S(1)} fusion(s32[1280]{0:T(1024)S(1)} %iota_add_fusion.2, s32[1024]{0:T(1024)S(1)} %iota_and_fusion, s32[1024]{0:T(1024)S(1)} %fusion.242, pred[1024]{0:T(1024)(128)(4,1)S(1)} %get-tuple-element.53, pred[1024]{0:T(1024)(128)(4,1)S(1)} %get-tuple-element.52, f32[2,1280,256]{1,2,0:T(8,128)S(1)} %fusion.348), kind=kOutput, calls=%fused_computation.110 | convolution fusion | flops 8071413760 | bytes 4733952 | tf_op jit(solution)/shard_map/nxc,xk->nck/dot_general | solution.py:75
  633.6 31.2 %fusion.80 = f32[2,256,1024]{2,1,0:T(8,128)S(1)} fusion(s32[1280]{0:T(1024)S(1)} %iota_add_fusion, s32[1024]{0:T(1024)S(1)} %iota_and_fusion, s32[1024]{0:T(1024)S(1)} %fusion.242, pred[1024]{0:T(1024)(128)(4,1)S(1)} %get-tuple-element.53, pred[1024]{0:T(1024)(128)(4,1)S(1)} %get-tuple-element.52, f32[2,1280,256]{1,2,0:T(8,128)S(1)} %fusion.344), kind=kOutput, calls=%fused_computation.106 | convolution fusion | flops 8071413760 | bytes 4733952 | tf_op jit(solution)/shard_map/nxc,xk->nck/dot_general | solution.py:75
  664.8 31.2 %add_add_fusion = f32[2,256,1024]{2,1,0:T(8,128)} fusion(f32[2,256,1024]{2,1,0:T(8,128)S(1)} %fusion.80, f32[2,256,1024]{2,1,0:T(8,128)S(1)} %fusion.82, f32[2,256,1024]{2,1,0:T(8,128)S(1)} %fusion.84, s32[1024]{0:T(1024)S(1)} %iota_and_fusion, s32[1024]{0:T(1024)S(1)} %fusion.242, pred[1024]{0:T(1024)(128)(4,1)S(1)} %get-tuple-element.53, ...), kind=kOutput, calls=%fused_computation.256 | convolution fusion | flops 8072986624 | bytes 11020288 | tf_op jit(solution)/shard_map/nxc,xk->nck/dot_general | solution.py:75
  696.0 3.3 reshape.162
  699.3 1.5 fusion.312
  701.0 0.1 maximum_multiply_fusion.1
  701.1 0.6 gather_fusion
  701.7 1.2 broadcast_select_fusion
  703.2 0.1 fusion.245
  703.5 0.2 bitcast_select_fusion
  703.8 80.2 %all-gather.2.cloned.1.call-done = f32[8,2,128,512]{3,2,1,0:T(8,128)} async-done(((f32[2,2,128,512]{3,2,1,0:T(8,128)}), f32[8,2,128,512]{3,2,1,0:T(8,128)}) %all-gather.2.cloned.1.call-update) | async-done | bytes 4194320 | tf_op jit(solution)/shard_map/all_gather | solution.py:100
  784.0 5.0 gather_fusion.1
  789.1 5.0 gather_fusion.2
  794.1 4.7 multiply_add_fusion
  798.8 2.6 maximum_select_fusion
  801.4 2.6 fusion.120
  (47 shorter events, 0.9 us)
Async XLA Ops:
  415.0 5.6 copy-start.2
  415.0 122.5 %all-to-all-start = ((f32[2,640,2048]{1,0,2:T(2,128)}), f32[2,640,2048]{1,0,2:T(2,128)}, u32[]{:S(2)}, u32[]{:S(2)}) async-start(f32[2,640,2048]{1,0,2:T(2,128)} %reshape.161), calls=%async_computation | async-start | bytes 20971520 | tf_op jit(solution)/shard_map/all_to_all | solution.py:71
  420.3 363.8 %all-gather.2.cloned.1.call-start = ((), (), s32[]{:S(2)}) async-start(), calls=%async_computation.1 | async-start | bytes 5242880 | tf_op jit(solution)/shard_map/all_gather | solution.py:100
  700.8 2.4 copy-start
  798.8 2.6 copy-start.1
Sparse Core Ops, SparseCore 0:
  703.1 80.9 all-gather.1
where the time goes:
time: 817 us; the launch traced here: 811 us
  matrix products  515 us (63%)
  waiting for transfers between devices  197 us (24%)
  local copies, waits for them, and re-layouts  62.5 us (8%)
  other arithmetic  16.6 us (2%)
  between operations  14.7 us (2%)
    dot_general x4, matrix products, local(): jnp.dot(flat_field, spanwise_table(first_col, col_block, mode_share), pre...  390 us
    dot_general x4, matrix products, local(): jnp.einsum('nxc,xk->nck', items[:, first_row:first_row + row_block], axia...  125 us
    all_to_all x1, waiting for transfers between devices, local(): lax.all_to_all(halfway, 'pencil', split_axis=2, concat_axis=1, tiled=True)  117 us
    all_gather x1, waiting for transfers between devices, local(): everything = lax.all_gather(spectra, 'plane', axis=0, tiled=True)  80.2 us
    all_to_all x2, local copies, waits for them, and re-layouts, local(): lax.all_to_all(halfway, 'pencil', split_axis=2, concat_axis=1, tiled=True)  25.9 us
  transfers between devices with their start and end apart: 2, of which 2 were waited for; matrix products, arithmetic and copies ran while one was open for 0% of the time, Pallas kernels for 0%

commit v1 on v0

v1 whole, which is shorter than its diff:
```python
import functools
import math

import ml_dtypes
import numpy as np

import jax
import jax.numpy as jnp
from jax import lax
from jax.experimental import pallas as pl
from jax.experimental.pallas import tpu as pltpu
from jax.sharding import PartitionSpec as P

KX = 512
KZ = 1024
F32 = jnp.float32
BF16 = jnp.bfloat16


def split_table(table):
    high = table.astype(np.float32).astype(ml_dtypes.bfloat16)
    low = (table - high.astype(np.float64)).astype(np.float32).astype(ml_dtypes.bfloat16)
    return high, low


def span_tables(nz, shares, chunks):
    per_owner = KZ // shares
    per_chunk = per_owner // chunks
    mode = np.arange(KZ).reshape(shares, chunks, per_chunk // 2, 2)
    mode = mode.transpose(1, 3, 0, 2)
    angle = (mode[..., None] * np.arange(nz // 2) % nz) * (2.0 * math.pi / nz)
    parts = np.stack([np.cos(angle), -np.sin(angle)], axis=2)
    high, low = split_table(parts)
    return np.stack([high, low], axis=2)


def axial_tables(nx, nz, shares):
    pos = np.arange(nx).reshape(shares, nx // shares)
    column = np.arange(KX // 2)
    angle = ((2 * column + 1) * pos[..., None] % (2 * nx)) * (math.pi / nx)
    table = np.concatenate([np.cos(angle), np.sin(angle)], axis=-1) / math.sqrt(nx * nz)
    high, low = split_table(table)
    shift = np.stack([np.cos(pos * math.pi / nx), np.sin(pos * math.pi / nx)], axis=1)
    return np.stack([high, low], axis=1), shift.astype(np.float32)


def halving_orders(shares):
    bits = list(range(1, shares.bit_length() - 1))
    middle = len(bits) // 2
    return bits, bits[middle:] + bits[:middle]


def relative(index, order):
    top = len(order) - 1
    return sum(((index >> (top - step)) & 1) << bit for step, bit in enumerate(order))


def owner_table(shares):
    orders = halving_orders(shares)
    rows = []
    for me in range(shares):
        other = me ^ 1
        sent = [other ^ relative(i, orders[other & 1]) for i in range(shares // 2)]
        kept = [me ^ relative(i, orders[me & 1]) for i in range(shares // 2)]
        rows.append([me] + sent + kept)
    return np.array(rows, np.int32)


def split(value):
    high = value.astype(BF16)
    return high, (value - high.astype(F32)).astype(BF16)


def dot_nt(left, right):
    return lax.dot_general(left, right, (((1,), (1,)), ((), ())), preferred_element_type=F32)


def dot_nn(left, right):
    return lax.dot_general(left, right, (((1,), (0,)), ((), ())), preferred_element_type=F32)


def transform_kernel(planes, rows, shares, meta, field, span, axial, shift, sent, kept, y_high, y_low):
    tile = field.shape[0]
    half = field.shape[1] // 2
    modes = span.shape[5]
    per_part = shares * modes
    step = pl.program_id(0)
    first = field[:, :half]
    second = field[:, half:]
    cos_shift = shift[0, 0:1, :]
    sin_shift = shift[0, 1:2, :]
    for parity in range(2):
        high, low = split(first + second if parity == 0 else first - second)
        table = span[0, parity].reshape(2 * 2 * per_part, half)
        both = dot_nt(table, high)
        value = both[: 2 * per_part] + both[2 * per_part :] + dot_nt(table[: 2 * per_part], low)
        re_part = value[:per_part]
        im_part = value[per_part:]
        turned = (
            re_part * cos_shift - im_part * sin_shift,
            re_part * sin_shift + im_part * cos_shift,
        )
        for part in range(2):
            high, low = split(turned[part])
            y_high[step, parity, part] = high.reshape(shares, modes, tile)
            y_low[step, parity, part] = low.reshape(shares, modes, tile)

    @pl.when(step == pl.num_programs(0) - 1)
    def _():
        half_count = shares // 2
        for plane in range(planes):
            pieces = []
            for index in range(planes * rows // tile):
                start = max(plane * rows, index * tile)
                stop = min((plane + 1) * rows, (index + 1) * tile)
                if start < stop:
                    pieces.append((index, start - index * tile, stop - index * tile))
            for target, base in ((sent, 1), (kept, 1 + half_count)):

                def gather(source):
                    blocks = []
                    for item in range(half_count):
                        owner = meta[base + item]
                        for parity in range(2):
                            for part in range(2):
                                blocks.append(
                                    jnp.concatenate(
                                        [
                                            source[index, parity, part, owner][:, lo:hi]
                                            for index, lo, hi in pieces
                                        ],
                                        axis=1,
                                    )
                                )
                    return jnp.concatenate(blocks, axis=0)

                left = gather(y_high)
                total = dot_nn(left, axial[0, 0]) + dot_nn(left, axial[0, 1])
                total = total + dot_nn(gather(y_low), axial[0, 0])
                target[:, plane] = total.reshape(half_count, 2, 2, modes, KX)


def transform(meta, field, span, axial, shift, chunk, planes):
    shares = axial.shape[0]
    rows = axial.shape[2]
    nz = field.shape[1]
    modes = span.shape[5]
    tile = 256 if rows % 128 == 0 and planes * rows % 256 == 0 else rows
    steps = planes * rows // tile
    out = jax.ShapeDtypeStruct((shares // 2, planes, 2, 2, modes, KX), F32)
    out_spec = pl.BlockSpec(out.shape, lambda i, meta: (0,) * 6)
    table_rows = 4 * shares * modes
    return pl.pallas_call(
        functools.partial(transform_kernel, planes, rows, shares),
        out_shape=(out, out),
        grid_spec=pltpu.PrefetchScalarGridSpec(
            num_scalar_prefetch=1,
            grid=(steps,),
            in_specs=[
                pl.BlockSpec((tile, nz), lambda i, meta: (i, 0)),
                pl.BlockSpec(
                    (1,) + span.shape[1:],
                    lambda i, meta: (chunk, 0, 0, 0, 0, 0, 0),
                    pipeline_mode=pl.Buffered(1),
                ),
                pl.BlockSpec((1,) + axial.shape[1:], lambda i, meta: (meta[0], 0, 0, 0), pipeline_mode=pl.Buffered(1)),
                pl.BlockSpec((1, 2, tile), lambda i, meta: (i, 0, 0)),
            ],
            out_specs=(out_spec, out_spec),
            scratch_shapes=[pltpu.VMEM((steps, 2, 2, shares, modes, tile), BF16)] * 2,
        ),
        compiler_params=pltpu.CompilerParams(vmem_limit_bytes=56 * 1024 * 1024),
        cost_estimate=pl.CostEstimate(
            flops=6 * planes * rows * table_rows * (nz // 2 + KX),
            bytes_accessed=planes * rows * nz * 4 + table_rows * nz * 2 + table_rows * planes * KX * 2,
            transcendentals=0,
        ),
        name="transform",
    )(meta, field, span, axial, shift)


def combine_kernel(count, scalars, *refs):
    terms, out, woven = refs[:count], refs[count], refs[count + 1]
    modes = terms[0].shape[4]
    half = KX // 2
    row = lax.broadcasted_iota(jnp.int32, (half, half), 0)
    column = lax.broadcasted_iota(jnp.int32, (half, half), 1)
    mirror = (row + column == half - 1).astype(BF16)

    def mirrored(value):
        high, rest = split(value)
        middle = value - high.astype(F32)
        middle, low = split(middle)
        return dot_nn(high, mirror) + dot_nn(middle, mirror) + dot_nn(low, mirror)

    for parity in range(2):
        re_rows, im_rows = (
            functools.reduce(lambda a, b: a + b, [term[0, 0, parity, part] for term in terms])
            for part in range(2)
        )
        re_cos, re_sin = re_rows[:, :half], re_rows[:, half:]
        im_cos, im_sin = im_rows[:, :half], im_rows[:, half:]
        values = (
            (re_cos + im_sin, mirrored(re_cos - im_sin)),
            (im_cos - re_sin, mirrored(im_cos + re_sin)),
        )
        for part in range(2):
            for side in range(2):
                for group in range(half // 128):
                    woven[part, side * (half // 128) + group, pl.ds(parity, modes, stride=2), :] = values[part][side][
                        :, group * 128 : (group + 1) * 128
                    ]
    for part in range(2):
        for group in range(KX // 128):
            out[0, part, :, group * 128 : (group + 1) * 128] = woven[part, group]


def combine(scalars, terms, planes):
    modes = terms[0].shape[4]
    spec = pl.BlockSpec(
        (1, 1, 2, 2, modes, KX), lambda i, scalars: (0, scalars[1 + i], 0, 0, 0, 0)
    )
    return pl.pallas_call(
        functools.partial(combine_kernel, len(terms)),
        out_shape=jax.ShapeDtypeStruct((planes, 2, 2 * modes, KX), F32),
        grid_spec=pltpu.PrefetchScalarGridSpec(
            num_scalar_prefetch=1,
            grid=(planes,),
            in_specs=[spec] * len(terms),
            out_specs=pl.BlockSpec((1, 2, 2 * modes, KX), lambda i, scalars: (i, 0, 0, 0)),
            scratch_shapes=[pltpu.VMEM((2, KX // 128, 2 * modes, 128), F32)],
        ),
        cost_estimate=pl.CostEstimate(
            flops=planes * modes * KX * 40, bytes_accessed=planes * modes * KX * 16 * (len(terms) + 1), transcendentals=0
        ),
        name="combine",
    )(scalars, *terms)


def cross_kernel(planes, band, reach, aliased, scalars, pairs, *refs):
    sources = refs[: 1 + 2 * reach]
    band_out, partner_out, wanted = refs[1 + 2 * reach + 2 * aliased :]

    def plane_value(offset):
        if 0 <= offset < planes:
            ref, index = sources[0], offset
        elif offset < 0:
            away = -(offset // planes)
            ref, index = sources[away], offset + away * planes - (1 if away == reach else 0)
        else:
            away = offset // planes
            ref, index = sources[reach + away], offset - away * planes
        return ref[index, 0], ref[index, 1]

    @pl.when(pl.program_id(0) == 0)
    def _():
        first_plane = scalars[0]

        def clear(index, carry):
            wanted[index] = 0
            return carry

        lax.fori_loop(0, 2 * planes * band, clear, 0)

        def mark(index, carry):
            lower = pairs[2 * index]
            upper = pairs[2 * index + 1]
            gap = upper - lower
            for side, plane in enumerate((lower - first_plane, upper - first_plane)):

                @pl.when((plane >= 0) & (plane < planes))
                def _():
                    wanted[(side * planes + plane) * band + gap] = 1

            return carry

        lax.fori_loop(0, pairs.shape[0] // 2, mark, 0)

    values = {offset: plane_value(offset) for offset in range(1 - band, planes + band - 1)}
    for own in range(planes):
        own_re, own_im = values[own]
        for gap in range(band):
            keep = wanted[own * band + gap] != 0
            far_re, far_im = values[own + gap]
            band_out[own, gap, 0] = jnp.where(keep, own_re * far_re + own_im * far_im, 0.0)
            band_out[own, gap, 1] = jnp.where(keep, own_im * far_re - own_re * far_im, 0.0)
            keep = wanted[(planes + own) * band + gap] != 0
            far_re, far_im = values[own - gap]
            partner_out[own, gap, 0] = jnp.where(keep, far_re * own_re + far_im * own_im, 0.0)
            partner_out[own, gap, 1] = jnp.where(keep, far_re * own_im - far_im * own_re, 0.0)


def cross(scalars, pairs, sources, earlier, planes, band, reach, chunk, chunks):
    rows = sources[0].shape[2]
    block = min(rows, 16)
    steps = rows // block
    out = jax.ShapeDtypeStruct((planes, band, 2, chunks * rows, KX), F32)
    out_spec = pl.BlockSpec((planes, band, 2, block, KX), lambda i, *s: (0, 0, 0, chunk * steps + i, 0))
    specs = [pl.BlockSpec((source.shape[0], 2, block, KX), lambda i, *s: (0, 0, i, 0)) for source in sources]
    specs += [pl.BlockSpec(memory_space=pl.ANY)] * len(earlier)
    return pl.pallas_call(
        functools.partial(cross_kernel, planes, band, reach, 1 if earlier else 0),
        out_shape=(out, out),
        grid_spec=pltpu.PrefetchScalarGridSpec(
            num_scalar_prefetch=2,
            grid=(steps,),
            in_specs=specs,
            out_specs=(out_spec, out_spec),
            scratch_shapes=[pltpu.SMEM((2 * planes * band,), jnp.int32)],
        ),
        input_output_aliases={2 + len(sources) + i: i for i in range(len(earlier))},
        cost_estimate=pl.CostEstimate(
            flops=planes * band * rows * KX * 12,
            bytes_accessed=(planes * band * 4 + 2 * (planes + 2 * band)) * rows * KX * 4,
            transcendentals=0,
        ),
        name="cross",
    )(scalars, pairs, *sources, *earlier)


def solution(mesh):
    shares = mesh.shape["pencil"]
    slabs = mesh.shape["plane"]
    reach = slabs // 2
    orders = halving_orders(shares)
    share = KZ // shares
    chunks = 2 if share % 64 == 0 else 1
    core_swap = [(i, i ^ 1) for i in range(shares)]
    swaps = [
        [(i, i ^ (1 << orders[i & 1][step])) for i in range(shares)] for step in range(len(orders[0]))
    ]
    upward = [(i, i + 1) for i in range(slabs - 1)]
    downward = [(i + 1, i) for i in range(slabs - 1)]

    def local(velocity, plane_slot, pair_list):
        planes, rows, nz = velocity.shape
        band = planes * reach
        span = span_tables(nz, shares, chunks)
        axial, shift = axial_tables(rows * shares, nz, shares)
        me = lax.axis_index("pencil")
        meta = lax.dynamic_index_in_dim(jnp.asarray(owner_table(shares)), me, 0, keepdims=False)
        tile = 256 if rows % 128 == 0 and planes * rows % 256 == 0 else rows
        mine = lax.dynamic_index_in_dim(jnp.asarray(shift), me, 0, keepdims=False)
        mine = jnp.tile(mine, (1, planes)).reshape(2, planes * rows // tile, tile).transpose(1, 0, 2)
        first_plane = lax.axis_index("plane") * planes
        held = lax.dynamic_slice_in_dim(plane_slot, first_plane, planes, 0) - first_plane
        scalars = jnp.concatenate([first_plane[None], held]).astype(jnp.int32)
        pairs = pair_list.reshape(-1)
        field = velocity.reshape(planes * rows, nz)

        def reduced(chunk):
            sent, kept = transform(meta, field, span, axial, mine, chunk, planes)
            terms = [kept, lax.ppermute(sent, "pencil", core_swap)]
            count = shares // 2
            for swap in swaps:
                count //= 2
                leaving = functools.reduce(lambda a, b: a + b, [term[count : 2 * count] for term in terms])
                terms.append(lax.ppermute(leaving, "pencil", swap))
            return combine(scalars, terms, planes)

        outputs = ()
        for chunk in range(chunks):
            own = reduced(chunk)
            below, above = [own], [own]
            for away in range(1, reach + 1):
                last = away == reach
                low, high = below[-1], above[-1]
                below.append(lax.ppermute(low[1:] if last else low, "plane", upward))
                above.append(lax.ppermute(high[:-1] if last else high, "plane", downward))
            outputs = cross(
                scalars, pairs, below + above[1:], outputs, planes, band, reach, chunk, chunks
            )
        return tuple(outputs)

    return jax.shard_map(
        local,
        mesh=mesh,
        in_specs=(P("plane", "pencil", None), P(), P()),
        out_specs=(P("plane", None, None, "pencil", None), P("plane", None, None, "pencil", None)),
        check_vma=False,
    )
```

time: 817 us -> 152 us (0.19)
  matrix products: 515 us -> 0 us
  waiting for transfers between devices: 197 us -> 29.4 us
  Pallas kernels: 0 us -> 78.3 us
  local copies, waits for them, and re-layouts: 62.5 us -> 6.49 us
  starting transfers between devices: 5.55 us -> 34.4 us
  other arithmetic: 16.6 us -> 1.44 us
  between operations: 14.7 us -> 0.87 us
    dot_general x8 -> x0, matrix products: 515 us -> none  [the longest x4 390 us: local(): jnp.dot(flat_field, spanwise_table(first_col, col_block, mode_share), pre...]
    all_to_all x1 -> x0, waiting for transfers between devices: 117 us -> none  [local(): lax.all_to_all(halfway, 'pencil', split_axis=2, concat_axis=1, tiled=True)]
    all_gather x1 -> x0, waiting for transfers between devices: 80.2 us -> none  [local(): everything = lax.all_gather(spectra, 'plane', axis=0, tiled=True)]
    pallas_call x0 -> x6, Pallas kernels: none -> 78.3 us  [the longest x2 61.4 us: transform(): pl.pallas_call(functools.partial(transform_kernel, planes, rows, shares),...]
    ppermute x0 -> x14, starting transfers between devices: none -> 34.4 us  [the longest x4 19 us: local(): below.append(lax.ppermute(low[1:] if last else low, 'plane', upward))]
    ppermute x0 -> x14, waiting for transfers between devices: none -> 29.4 us  [the longest x4 23.4 us: reduced(): terms.append(lax.ppermute(leaving, 'pencil', swap))]
    all_to_all x2 -> x0, local copies, waits for them, and re-layouts: 25.9 us -> none  [local(): lax.all_to_all(halfway, 'pencil', split_axis=2, concat_axis=1, tiled=True)]
    reshape x2 -> x1, local copies, waits for them, and re-layouts: 16.4 us -> 0.61 us  [local(): pairs = pair_list.reshape(-1)]
  transfers between devices with their start and end apart: 2 -> 14, of which waited for: 2 -> 5; matrix products, arithmetic and copies ran while one was open for 0% -> 2% of each run, Pallas kernels for 0% -> 28%
where the time goes in v1:
time: 152 us; the launch traced here: 151 us
  Pallas kernels  78.3 us (52%)
  starting transfers between devices  34.4 us (23%)
  waiting for transfers between devices  29.4 us (19%)
  local copies, waits for them, and re-layouts  6.49 us (4%)
    pallas_call x2, Pallas kernels, transform(): pl.pallas_call(functools.partial(transform_kernel, planes, rows, shares),...  61.4 us
    ppermute x4, waiting for transfers between devices, reduced(): terms.append(lax.ppermute(leaving, 'pencil', swap))  23.4 us
    ppermute x4, starting transfers between devices, local(): below.append(lax.ppermute(low[1:] if last else low, 'plane', upward))  19 us
    pallas_call x2, Pallas kernels, cross(): pl.pallas_call(functools.partial(cross_kernel, planes, band, reach, 1 if...  10 us
    ppermute x4, starting transfers between devices, reduced(): terms.append(lax.ppermute(leaving, 'pencil', swap))  9.65 us
    pallas_call x2, Pallas kernels, combine(): pl.pallas_call(functools.partial(combine_kernel, len(terms)), out_shape=j...  6.91 us
    ppermute x4, starting transfers between devices, local(): above.append(lax.ppermute(high[:-1] if last else high, 'plane', downward))  5.28 us
    ppermute x4, waiting for transfers between devices, local(): above.append(lax.ppermute(high[:-1] if last else high, 'plane', downward))  4.79 us
  transfers between devices with their start and end apart: 14, of which 5 were waited for; matrix products, arithmetic and copies ran while one was open for 2% of the time, Pallas kernels for 28%

profile of v1, /device:TPU:0, one launch (start us, length us, event | category | flops | bytes accessed | tf_op | source)
XLA Modules:
  0.0 150.9 jit_solution(9080130603493652732)
XLA Ops:
  0.6 1.3 dynamic-slice_bitcast_fusion.1.meta
  1.9 0.7 dynamic-slice_bitcast_fusion
  2.6 0.6 copy.15
  3.2 30.7 %transform.3 = (f32[4,2,2,2,32,512]{5,4,3,2,1,0:T(8,128)}, f32[4,2,2,2,32,512]{5,4,3,2,1,0:T(8,128)}) custom-call(s32[9]{0:T(128)} %dynamic-slice_bitcast_fusion.1.meta, f32[1280,3840]{1,0:T(8,128)} %bitcast.11, bf16[2,2,2,2,8,32,1920]{6,5,4,3,2,1,0:T(8,128)(2,1)} %constant.32.clone.span, bf16[8,2,640,512]{3,2,1,0:T(8,128)(2,1)} %constant.33.clone.axial, ...), custom_call_target="tpu_custom_call" | custom-call | flops 19126026240 | bytes 29622272 | tf_op jit(solution)/shard_map/transform/pallas_call | solution.py:153
  33.9 0.4 collective-permute-start.7
  34.3 30.7 %transform.2 = (f32[4,2,2,2,32,512]{5,4,3,2,1,0:T(8,128)}, f32[4,2,2,2,32,512]{5,4,3,2,1,0:T(8,128)}) custom-call(s32[9]{0:T(128)} %dynamic-slice_bitcast_fusion.1.meta, f32[1280,3840]{1,0:T(8,128)} %bitcast.12, bf16[2,2,2,2,8,32,1920]{6,5,4,3,2,1,0:T(8,128)(2,1)} %constant.32.clone.span, bf16[8,2,640,512]{3,2,1,0:T(8,128)(2,1)} %constant.33.clone.axial, ...), custom_call_target="tpu_custom_call" | custom-call | flops 19126026240 | bytes 29622272 | tf_op jit(solution)/shard_map/transform/pallas_call | solution.py:153
  65.4 2.9 %collective-permute-start.8 = (f32[2,2,2,2,32,512]{5,4,3,2,1,0:T(8,128)S(1)}, f32[2,2,2,2,32,512]{5,4,3,2,1,0:T(8,128)S(1)}, u32[]{:S(2)}, u32[]{:S(2)}) collective-permute-start(f32[2,2,2,2,32,512]{5,4,3,2,1,0:T(8,128)S(1)} %slice_add_fusion), channel_id=1, source_target_pairs={{0,2},{1,5},{2,0},{3,7},{4,6},{5,1},{6,4},{7,3},{8,10},{9,13},{10,... | collective-permute-start | bytes 3145736 | tf_op jit(solution)/shard_map/ppermute | solution.py:358
  68.2 1.2 collective-permute-done.refs_1_
  69.7 2.6 %collective-permute-start.1 = (f32[2,2,2,2,32,512]{5,4,3,2,1,0:T(8,128)S(1)}, f32[2,2,2,2,32,512]{5,4,3,2,1,0:T(8,128)S(1)}, u32[]{:S(2)}, u32[]{:S(2)}) collective-permute-start(f32[2,2,2,2,32,512]{5,4,3,2,1,0:T(8,128)S(1)} %slice_add_fusion.1), channel_id=1, source_target_pairs={{0,2},{1,5},{2,0},{3,7},{4,6},{5,1},{6,4},{7,3},{8,10},{9,13},{10,... | collective-permute-start | bytes 3145736 | tf_op jit(solution)/shard_map/ppermute | solution.py:358
  72.2 8.8 %collective-permute-done.8.refs_2_ = f32[2,2,2,2,32,512]{5,4,3,2,1,0:T(8,128)S(1)} collective-permute-done((f32[2,2,2,2,32,512]{5,4,3,2,1,0:T(8,128)S(1)}, f32[2,2,2,2,32,512]{5,4,3,2,1,0:T(8,128)S(1)}, u32[]{:S(2)}, u32[]{:S(2)}) %collective-permute-start.8) | collective-permute-done | bytes 1048608 | tf_op jit(solution)/shard_map/ppermute | solution.py:358
  81.2 2.1 %collective-permute-start.9 = (f32[1,2,2,2,32,512]{5,4,3,2,1,0:T(8,128)S(1)}, f32[1,2,2,2,32,512]{5,4,3,2,1,0:T(8,128)S(1)}, u32[]{:S(2)}, u32[]{:S(2)}) collective-permute-start(f32[1,2,2,2,32,512]{5,4,3,2,1,0:T(8,128)S(1)} %slice_add_fusion.2), channel_id=1, source_target_pairs={{0,4},{1,3},{2,6},{3,1},{4,0},{5,7},{6,2},{7,5},{8,12},{9,11},{10,... | collective-permute-start | bytes 1572872 | tf_op jit(solution)/shard_map/ppermute | solution.py:358
  83.3 14.6 %collective-permute-done.1.refs_2_ = f32[2,2,2,2,32,512]{5,4,3,2,1,0:T(8,128)S(1)} collective-permute-done((f32[2,2,2,2,32,512]{5,4,3,2,1,0:T(8,128)S(1)}, f32[2,2,2,2,32,512]{5,4,3,2,1,0:T(8,128)S(1)}, u32[]{:S(2)}, u32[]{:S(2)}) %collective-permute-start.1) | collective-permute-done | bytes 1048608 | tf_op jit(solution)/shard_map/ppermute | solution.py:358
  98.0 2.1 %collective-permute-start.2 = (f32[1,2,2,2,32,512]{5,4,3,2,1,0:T(8,128)S(1)}, f32[1,2,2,2,32,512]{5,4,3,2,1,0:T(8,128)S(1)}, u32[]{:S(2)}, u32[]{:S(2)}) collective-permute-start(f32[1,2,2,2,32,512]{5,4,3,2,1,0:T(8,128)S(1)} %slice_add_fusion.4), channel_id=1, source_target_pairs={{0,4},{1,3},{2,6},{3,1},{4,0},{5,7},{6,2},{7,5},{8,12},{9,11},{10,... | collective-permute-start | bytes 1572872 | tf_op jit(solution)/shard_map/ppermute | solution.py:358
  100.2 0.6 pad_add_fusion.scalars
  100.8 0.8 copy-done.11
  101.6 3.5 %combine.3.refs_0_ = f32[2,2,64,512]{3,2,1,0:T(8,128)} custom-call(s32[3]{0:T(128)} %pad_add_fusion.scalars, f32[4,2,2,2,32,512]{5,4,3,2,1,0:T(8,128)} %get-tuple-element.10.refs_0_, f32[4,2,2,2,32,512]{5,4,3,2,1,0:T(8,128)} %copy-done.3, f32[2,2,2,2,32,512]{5,4,3,2,1,0:T(8,128)} %copy-done.5, f32[1,2,2,2,32,512]{5,4,3,2,1,0:T(8,128)} %copy-done.11), custom_call_target="tpu_custom_call" | custom-call | flops 1310720 | bytes 2621440 | tf_op jit(solution)/shard_map/combine/pallas_call | solution.py:223
  105.1 1.3 collective-permute-start.12
  106.4 4.6 %collective-permute-start.10 = (f32[2,2,64,512]{3,2,1,0:T(8,128)}, f32[2,2,64,512]{3,2,1,0:T(8,128)S(1)}, u32[]{:S(2)}, u32[]{:S(2)}) collective-permute-start(f32[2,2,64,512]{3,2,1,0:T(8,128)} %combine.3.refs_0_), channel_id=1, source_target_pairs={{0,8},{8,16},{16,24},{1,9},{9,17},{17,25},{2,10},{10,18},{18,26},{... | collective-permute-start | bytes 1572872 | tf_op jit(solution)/shard_map/ppermute | solution.py:368
  111.0 0.8 copy-done.10
  111.8 3.5 %combine.2.refs_0_ = f32[2,2,64,512]{3,2,1,0:T(8,128)} custom-call(s32[3]{0:T(128)} %pad_add_fusion.scalars, f32[4,2,2,2,32,512]{5,4,3,2,1,0:T(8,128)} %get-tuple-element.8.refs_0_, f32[4,2,2,2,32,512]{5,4,3,2,1,0:T(8,128)} %copy-done.1, f32[2,2,2,2,32,512]{5,4,3,2,1,0:T(8,128)} %copy-done.4, f32[1,2,2,2,32,512]{5,4,3,2,1,0:T(8,128)} %copy-done.10), custom_call_target="tpu_custom_call" | custom-call | flops 1310720 | bytes 2621440 | tf_op jit(solution)/shard_map/combine/pallas_call | solution.py:223
  115.2 1.4 collective-permute-start.5
  116.6 4.6 %collective-permute-start.3 = (f32[2,2,64,512]{3,2,1,0:T(8,128)}, f32[2,2,64,512]{3,2,1,0:T(8,128)S(1)}, u32[]{:S(2)}, u32[]{:S(2)}) collective-permute-start(f32[2,2,64,512]{3,2,1,0:T(8,128)} %combine.2.refs_0_), channel_id=1, source_target_pairs={{0,8},{8,16},{16,24},{1,9},{9,17},{17,25},{2,10},{10,18},{18,26},{... | collective-permute-start | bytes 1572872 | tf_op jit(solution)/shard_map/ppermute | solution.py:368
  121.5 1.3 collective-permute-start.13
  122.8 5.3 %collective-permute-start.11 = (f32[1,2,64,512]{3,2,1,0:T(8,128)S(1)}, f32[1,2,64,512]{3,2,1,0:T(8,128)}, u32[]{:S(2)}, u32[]{:S(2)}) collective-permute-start(f32[1,2,64,512]{3,2,1,0:T(8,128)S(1)} %slice.64), channel_id=1, source_target_pairs={{0,8},{8,16},{16,24},{1,9},{9,17},{17,25},{2,10},{10,18},{18,26},{... | collective-permute-start | bytes 786440 | tf_op jit(solution)/shard_map/ppermute | solution.py:368
  128.1 4.6 %collective-permute-done.5.refs_3_ = f32[2,2,64,512]{3,2,1,0:T(8,128)S(1)} collective-permute-done((f32[2,2,64,512]{3,2,1,0:T(8,128)}, f32[2,2,64,512]{3,2,1,0:T(8,128)S(1)}, u32[]{:S(2)}, u32[]{:S(2)}) %collective-permute-start.5) | collective-permute-done | bytes 524320 | tf_op jit(solution)/shard_map/ppermute | solution.py:369
  132.7 1.3 collective-permute-start.6
  134.0 0.8 slice.59
  134.8 4.5 %collective-permute-start.4 = (f32[1,2,64,512]{3,2,1,0:T(8,128)}, f32[1,2,64,512]{3,2,1,0:T(8,128)S(1)}, u32[]{:S(2)}, u32[]{:S(2)}) collective-permute-start(f32[1,2,64,512]{3,2,1,0:T(8,128)} %slice.59), channel_id=1, source_target_pairs={{0,8},{8,16},{16,24},{1,9},{9,17},{17,25},{2,10},{10,18},{18,26},{... | collective-permute-start | bytes 786440 | tf_op jit(solution)/shard_map/ppermute | solution.py:368
  139.4 0.6 reshape.15.pairs
  140.1 5.0 %cross.2 = (f32[2,4,2,128,512]{4,3,2,1,0:T(8,128)}, f32[2,4,2,128,512]{4,3,2,1,0:T(8,128)}) custom-call(s32[3]{0:T(128)} %pad_add_fusion.scalars, s32[40]{0:T(128)} %reshape.15.pairs, f32[2,2,64,512]{3,2,1,0:T(8,128)} %combine.3.refs_0_, f32[2,2,64,512]{3,2,1,0:T(8,128)} %copy-done.7, f32[1,2,64,512]{3,2,1,0:T(8,128)} %collective-permute-done.11.refs_2_, ...), custom_call_target="tpu_custom_call" | custom-call | flops 3145728 | bytes 6815744 | tf_op jit(solution)/shard_map/cross/pallas_call | solution.py:301
  145.1 0.7 copy-done.12
  145.9 5.0 %cross.3 = (f32[2,4,2,128,512]{4,3,2,1,0:T(8,128)}, f32[2,4,2,128,512]{4,3,2,1,0:T(8,128)}) custom-call(s32[3]{0:T(128)} %pad_add_fusion.scalars, s32[40]{0:T(128)} %reshape.15.pairs, f32[2,2,64,512]{3,2,1,0:T(8,128)} %combine.2.refs_0_, f32[2,2,64,512]{3,2,1,0:T(8,128)} %copy-done.9, ...), custom_call_target="tpu_custom_call", output_to_operand_aliasing={{0}: (7, {}), {1}: (8, {})} | custom-call | flops 3145728 | bytes 6815744 | tf_op jit(solution)/shard_map/cross/pallas_call | solution.py:301
  (51 shorter events, 1.4 us)
Async XLA Ops:
  33.9 31.2 %copy-start.2 = (f32[4,2,2,2,32,512]{5,4,3,2,1,0:T(8,128)S(1)}, f32[4,2,2,2,32,512]{5,4,3,2,1,0:T(8,128)}, u32[]{:S(2)}) copy-start(f32[4,2,2,2,32,512]{5,4,3,2,1,0:T(8,128)} %get-tuple-element.10.refs_0_) | copy-start | bytes 6291460
  33.9 31.2 %collective-permute-start.7 = (f32[4,2,2,2,32,512]{5,4,3,2,1,0:T(8,128)}, f32[4,2,2,2,32,512]{5,4,3,2,1,0:T(8,128)S(1)}, u32[]{:S(2)}, u32[]{:S(2)}) collective-permute-start(f32[4,2,2,2,32,512]{5,4,3,2,1,0:T(8,128)} %get-tuple-element.11), channel_id=1, source_target_pairs={{0,1},{1,0},{2,3},{3,2},{4,5},{5,4},{6,7},{7,6},{8,9},{9,8},{10,11... | collective-permute-start | bytes 6291464 | tf_op jit(solution)/shard_map/ppermute | solution.py:353
  65.1 4.4 %copy-start = (f32[4,2,2,2,32,512]{5,4,3,2,1,0:T(8,128)S(1)}, f32[4,2,2,2,32,512]{5,4,3,2,1,0:T(8,128)}, u32[]{:S(2)}) copy-start(f32[4,2,2,2,32,512]{5,4,3,2,1,0:T(8,128)} %get-tuple-element.8.refs_0_) | copy-start | bytes 6291460
  65.1 4.4 %collective-permute-start = (f32[4,2,2,2,32,512]{5,4,3,2,1,0:T(8,128)}, f32[4,2,2,2,32,512]{5,4,3,2,1,0:T(8,128)S(1)}, u32[]{:S(2)}, u32[]{:S(2)}) collective-permute-start(f32[4,2,2,2,32,512]{5,4,3,2,1,0:T(8,128)} %get-tuple-element.9), channel_id=1, source_target_pairs={{0,1},{1,0},{2,3},{3,2},{4,5},{5,4},{6,7},{7,6},{8,9},{9,8},{10,11... | collective-permute-start | bytes 6291464 | tf_op jit(solution)/shard_map/ppermute | solution.py:353
  65.1 15.9 %copy-start.3 = (f32[4,2,2,2,32,512]{5,4,3,2,1,0:T(8,128)}, f32[4,2,2,2,32,512]{5,4,3,2,1,0:T(8,128)S(1)}, u32[]{:S(2)}) copy-start(f32[4,2,2,2,32,512]{5,4,3,2,1,0:T(8,128)S(1)} %collective-permute-done.7.refs_1_) | copy-start | bytes 6291460
  65.4 15.6 %collective-permute-start.8 = (f32[2,2,2,2,32,512]{5,4,3,2,1,0:T(8,128)S(1)}, f32[2,2,2,2,32,512]{5,4,3,2,1,0:T(8,128)S(1)}, u32[]{:S(2)}, u32[]{:S(2)}) collective-permute-start(f32[2,2,2,2,32,512]{5,4,3,2,1,0:T(8,128)S(1)} %slice_add_fusion), channel_id=1, source_target_pairs={{0,2},{1,5},{2,0},{3,7},{4,6},{5,1},{6,4},{7,3},{8,10},{9,13},{10,... | collective-permute-start | bytes 3145736 | tf_op jit(solution)/shard_map/ppermute | solution.py:358
  69.4 28.4 %copy-start.1 = (f32[4,2,2,2,32,512]{5,4,3,2,1,0:T(8,128)}, f32[4,2,2,2,32,512]{5,4,3,2,1,0:T(8,128)S(1)}, u32[]{:S(2)}) copy-start(f32[4,2,2,2,32,512]{5,4,3,2,1,0:T(8,128)S(1)} %collective-permute-done.refs_1_) | copy-start | bytes 6291460
  69.7 30.5 %copy-start.15 = (s32[8]{0:T(128)S(1)}, s32[8]{0:T(128)}, u32[]{:S(2)}) copy-start(s32[8]{0:T(128)} %param.8) | copy-start | bytes 100
  69.7 28.2 %collective-permute-start.1 = (f32[2,2,2,2,32,512]{5,4,3,2,1,0:T(8,128)S(1)}, f32[2,2,2,2,32,512]{5,4,3,2,1,0:T(8,128)S(1)}, u32[]{:S(2)}, u32[]{:S(2)}) collective-permute-start(f32[2,2,2,2,32,512]{5,4,3,2,1,0:T(8,128)S(1)} %slice_add_fusion.1), channel_id=1, source_target_pairs={{0,2},{1,5},{2,0},{3,7},{4,6},{5,1},{6,4},{7,3},{8,10},{9,13},{10,... | collective-permute-start | bytes 3145736 | tf_op jit(solution)/shard_map/ppermute | solution.py:358
  81.0 17.0 %copy-start.5 = (f32[2,2,2,2,32,512]{5,4,3,2,1,0:T(8,128)}, f32[2,2,2,2,32,512]{5,4,3,2,1,0:T(8,128)S(1)}, u32[]{:S(2)}) copy-start(f32[2,2,2,2,32,512]{5,4,3,2,1,0:T(8,128)S(1)} %collective-permute-done.8.refs_2_) | copy-start | bytes 3145732
  81.2 19.7 %collective-permute-start.9 = (f32[1,2,2,2,32,512]{5,4,3,2,1,0:T(8,128)S(1)}, f32[1,2,2,2,32,512]{5,4,3,2,1,0:T(8,128)S(1)}, u32[]{:S(2)}, u32[]{:S(2)}) collective-permute-start(f32[1,2,2,2,32,512]{5,4,3,2,1,0:T(8,128)S(1)} %slice_add_fusion.2), channel_id=1, source_target_pairs={{0,4},{1,3},{2,6},{3,1},{4,0},{5,7},{6,2},{7,5},{8,12},{9,11},{10,... | collective-permute-start | bytes 1572872 | tf_op jit(solution)/shard_map/ppermute | solution.py:358
  97.9 7.2 %copy-start.4 = (f32[2,2,2,2,32,512]{5,4,3,2,1,0:T(8,128)}, f32[2,2,2,2,32,512]{5,4,3,2,1,0:T(8,128)S(1)}, u32[]{:S(2)}) copy-start(f32[2,2,2,2,32,512]{5,4,3,2,1,0:T(8,128)S(1)} %collective-permute-done.1.refs_2_) | copy-start | bytes 3145732
  98.0 12.9 %collective-permute-start.2 = (f32[1,2,2,2,32,512]{5,4,3,2,1,0:T(8,128)S(1)}, f32[1,2,2,2,32,512]{5,4,3,2,1,0:T(8,128)S(1)}, u32[]{:S(2)}, u32[]{:S(2)}) collective-permute-start(f32[1,2,2,2,32,512]{5,4,3,2,1,0:T(8,128)S(1)} %slice_add_fusion.4), channel_id=1, source_target_pairs={{0,4},{1,3},{2,6},{3,1},{4,0},{5,7},{6,2},{7,5},{8,12},{9,11},{10,... | collective-permute-start | bytes 1572872 | tf_op jit(solution)/shard_map/ppermute | solution.py:358
  100.8 0.8 copy-start.11
  105.1 16.3 %collective-permute-start.12 = (f32[2,2,64,512]{3,2,1,0:T(8,128)}, f32[2,2,64,512]{3,2,1,0:T(8,128)S(1)}, u32[]{:S(2)}, u32[]{:S(2)}) collective-permute-start(f32[2,2,64,512]{3,2,1,0:T(8,128)} %combine.3.refs_0_), channel_id=1, source_target_pairs={{8,0},{16,8},{24,16},{9,1},{17,9},{25,17},{10,2},{18,10},{26,18},{... | collective-permute-start | bytes 1572872 | tf_op jit(solution)/shard_map/ppermute | solution.py:369
  106.4 16.4 %collective-permute-start.10 = (f32[2,2,64,512]{3,2,1,0:T(8,128)}, f32[2,2,64,512]{3,2,1,0:T(8,128)S(1)}, u32[]{:S(2)}, u32[]{:S(2)}) collective-permute-start(f32[2,2,64,512]{3,2,1,0:T(8,128)} %combine.3.refs_0_), channel_id=1, source_target_pairs={{0,8},{8,16},{16,24},{1,9},{9,17},{17,25},{2,10},{10,18},{18,26},{... | collective-permute-start | bytes 1572872 | tf_op jit(solution)/shard_map/ppermute | solution.py:368
  111.0 0.8 copy-start.10
  115.2 24.1 %copy-start.14 = (s32[20,2]{0,1:T(2,128)S(1)}, s32[20,2]{0,1:T(2,128)}, u32[]{:S(2)}) copy-start(s32[20,2]{0,1:T(2,128)} %param.9) | copy-start | bytes 484
  115.2 17.4 %collective-permute-start.5 = (f32[2,2,64,512]{3,2,1,0:T(8,128)}, f32[2,2,64,512]{3,2,1,0:T(8,128)S(1)}, u32[]{:S(2)}, u32[]{:S(2)}) collective-permute-start(f32[2,2,64,512]{3,2,1,0:T(8,128)} %combine.2.refs_0_), channel_id=1, source_target_pairs={{8,0},{16,8},{24,16},{9,1},{17,9},{25,17},{10,2},{18,10},{26,18},{... | collective-permute-start | bytes 1572872 | tf_op jit(solution)/shard_map/ppermute | solution.py:369
  116.6 17.3 %collective-permute-start.3 = (f32[2,2,64,512]{3,2,1,0:T(8,128)}, f32[2,2,64,512]{3,2,1,0:T(8,128)S(1)}, u32[]{:S(2)}, u32[]{:S(2)}) collective-permute-start(f32[2,2,64,512]{3,2,1,0:T(8,128)} %combine.2.refs_0_), channel_id=1, source_target_pairs={{0,8},{8,16},{16,24},{1,9},{9,17},{17,25},{2,10},{10,18},{18,26},{... | collective-permute-start | bytes 1572872 | tf_op jit(solution)/shard_map/ppermute | solution.py:368
  121.4 18.6 %copy-start.6 = (f32[2,2,64,512]{3,2,1,0:T(8,128)}, f32[2,2,64,512]{3,2,1,0:T(8,128)S(1)}, u32[]{:S(2)}) copy-start(f32[2,2,64,512]{3,2,1,0:T(8,128)S(1)} %collective-permute-done.12.refs_3_) | copy-start | bytes 1572868
  121.5 18.6 %collective-permute-start.13 = (f32[1,2,64,512]{3,2,1,0:T(8,128)S(1)}, f32[1,2,64,512]{3,2,1,0:T(8,128)}, u32[]{:S(2)}, u32[]{:S(2)}) collective-permute-start(f32[1,2,64,512]{3,2,1,0:T(8,128)S(1)} %slice.65), channel_id=1, source_target_pairs={{8,0},{16,8},{24,16},{9,1},{17,9},{25,17},{10,2},{18,10},{26,18},{... | collective-permute-start | bytes 786440 | tf_op jit(solution)/shard_map/ppermute | solution.py:369
  122.8 17.3 %copy-start.7 = (f32[2,2,64,512]{3,2,1,0:T(8,128)}, f32[2,2,64,512]{3,2,1,0:T(8,128)S(1)}, u32[]{:S(2)}) copy-start(f32[2,2,64,512]{3,2,1,0:T(8,128)S(1)} %collective-permute-done.10.refs_1_) | copy-start | bytes 1572868
  122.8 17.2 %collective-permute-start.11 = (f32[1,2,64,512]{3,2,1,0:T(8,128)S(1)}, f32[1,2,64,512]{3,2,1,0:T(8,128)}, u32[]{:S(2)}, u32[]{:S(2)}) collective-permute-start(f32[1,2,64,512]{3,2,1,0:T(8,128)S(1)} %slice.64), channel_id=1, source_target_pairs={{0,8},{8,16},{16,24},{1,9},{9,17},{17,25},{2,10},{10,18},{18,26},{... | collective-permute-start | bytes 786440 | tf_op jit(solution)/shard_map/ppermute | solution.py:368
  132.7 12.4 %copy-start.8 = (f32[2,2,64,512]{3,2,1,0:T(8,128)}, f32[2,2,64,512]{3,2,1,0:T(8,128)S(1)}, u32[]{:S(2)}) copy-start(f32[2,2,64,512]{3,2,1,0:T(8,128)S(1)} %collective-permute-done.5.refs_3_) | copy-start | bytes 1572868
  132.7 12.4 %collective-permute-start.6 = (f32[1,2,64,512]{3,2,1,0:T(8,128)S(1)}, f32[1,2,64,512]{3,2,1,0:T(8,128)S(1)}, u32[]{:S(2)}, u32[]{:S(2)}) collective-permute-start(f32[1,2,64,512]{3,2,1,0:T(8,128)S(1)} %slice.60), channel_id=1, source_target_pairs={{8,0},{16,8},{24,16},{9,1},{17,9},{25,17},{10,2},{18,10},{26,18},{... | collective-permute-start | bytes 786440 | tf_op jit(solution)/shard_map/ppermute | solution.py:369
  134.0 11.1 %copy-start.9 = (f32[2,2,64,512]{3,2,1,0:T(8,128)}, f32[2,2,64,512]{3,2,1,0:T(8,128)S(1)}, u32[]{:S(2)}) copy-start(f32[2,2,64,512]{3,2,1,0:T(8,128)S(1)} %collective-permute-done.3.refs_1_) | copy-start | bytes 1572868
  134.8 10.3 %collective-permute-start.4 = (f32[1,2,64,512]{3,2,1,0:T(8,128)}, f32[1,2,64,512]{3,2,1,0:T(8,128)S(1)}, u32[]{:S(2)}, u32[]{:S(2)}) collective-permute-start(f32[1,2,64,512]{3,2,1,0:T(8,128)} %slice.59), channel_id=1, source_target_pairs={{0,8},{8,16},{16,24},{1,9},{9,17},{17,25},{2,10},{10,18},{18,26},{... | collective-permute-start | bytes 786440 | tf_op jit(solution)/shard_map/ppermute | solution.py:368
  145.1 0.7 copy-start.12
  145.1 0.8 copy-start.13

commit v2 on v0

v2 whole, which is shorter than its diff:
```python
import functools
import math

import ml_dtypes
import numpy as np

import jax
import jax.numpy as jnp
from jax import lax
from jax.experimental import pallas as pl
from jax.experimental.pallas import tpu as pltpu
from jax.sharding import PartitionSpec as P

KX = 512
KZ = 1024
LANES = 128
GROUP = 8
F32 = jnp.float32
BF16 = jnp.bfloat16


def split_table(table):
    high = table.astype(np.float32).astype(ml_dtypes.bfloat16)
    low = (table - high.astype(np.float64)).astype(np.float32).astype(ml_dtypes.bfloat16)
    return high, low


def class_pairs(radix):
    return [(0, radix // 2)] + [(k, radix - k) for k in range(1, radix // 2)]


def span_table(nz, shares, radix):
    length = nz // radix
    padded = -(-length // LANES) * LANES
    per_owner = KZ // shares
    place = np.arange(length)
    pairs = []
    for number, pair in enumerate(class_pairs(radix)):
        table = np.zeros((2, shares, 2, GROUP, 2, padded))
        for member, residue in enumerate(pair):
            mode = np.arange(shares)[:, None] * per_owner + residue + radix * np.arange(GROUP)
            angle = (mode[..., None] * place % nz) * (2.0 * math.pi / nz)
            cosine, sine = np.cos(angle), np.sin(angle)
            if number == 0:
                table[0, :, member, :, member, :length] = cosine
                table[1, :, member, :, member, :length] = -sine
            else:
                sign = 1.0 if member == 0 else -1.0
                table[0, :, member, :, 0, :length] = cosine
                table[0, :, member, :, 1, :length] = sign * sine
                table[1, :, member, :, 0, :length] = -sine
                table[1, :, member, :, 1, :length] = sign * cosine
        pairs.append(table.reshape(2 * shares * 2 * GROUP, 2 * padded))
    high, low = split_table(np.stack(pairs))
    return np.concatenate([high, low], axis=1)


def axial_table(nx, nz, shares):
    pos = np.arange(nx).reshape(shares, nx // shares)
    column = np.arange(KX // 2)
    angle = ((2 * column + 1) * pos[..., None] % (2 * nx)) * (math.pi / nx)
    both = np.stack([np.cos(angle), np.sin(angle)], axis=2) / math.sqrt(nx * nz)
    both = both.reshape(shares, nx // shares, 2, -1, LANES).transpose(0, 1, 3, 2, 4)
    high, low = split_table(both.reshape(shares, nx // shares, KX))
    return np.concatenate([high, high, low], axis=1)


def shift_table(nx, shares):
    angle = np.arange(nx).reshape(shares, 1, nx // shares) * (math.pi / nx)
    rest = np.zeros((shares, 6, nx // shares))
    return np.concatenate([np.cos(angle), np.sin(angle), rest], axis=1).astype(np.float32)


def halving_orders(shares):
    bits = list(range(1, shares.bit_length() - 1))
    middle = len(bits) // 2
    return bits, bits[middle:] + bits[:middle]


def relative(index, order):
    top = len(order) - 1
    return sum(((index >> (top - step)) & 1) << bit for step, bit in enumerate(order))


def place_table(shares):
    orders = halving_orders(shares)
    rows = []
    for me in range(shares):
        other = me ^ 1
        sent = [other ^ relative(i, orders[other & 1]) for i in range(shares // 2)]
        kept = [me ^ relative(i, orders[me & 1]) for i in range(shares // 2)]
        rows.append(np.argsort(sent + kept))
    return np.array(rows, np.int32)


def split(value):
    high = value.astype(BF16)
    return high, (value - high.astype(F32)).astype(BF16)


def dot_nt(left, right):
    return lax.dot_general(left, right, (((1,), (1,)), ((), ())), preferred_element_type=F32)


def dot_nn(left, right):
    return lax.dot_general(left, right, (((1,), (0,)), ((), ())), preferred_element_type=F32)


def real_dft(values):
    count = len(values)
    if count == 1:
        return [(values[0], None)]
    if count == 2:
        return [(values[0] + values[1], None), (values[0] - values[1], None)]
    even = real_dft(values[0::2])
    odd = real_dft(values[1::2])
    out = [None] * (count // 2 + 1)
    for k in range(count // 4 + 1):
        even_re, even_im = even[k]
        odd_re, odd_im = odd[k]
        if k == 0:
            out[0] = (even_re + odd_re, None)
            out[count // 2] = (even_re - odd_re, None)
        elif 4 * k == count:
            out[k] = (even_re, -odd_re)
        else:
            cosine = math.cos(2.0 * math.pi * k / count)
            sine = math.sin(2.0 * math.pi * k / count)
            if 8 * k == count:
                turned_re = (odd_re + odd_im) * cosine
                turned_im = (odd_im - odd_re) * cosine
            else:
                turned_re = odd_re * cosine + odd_im * sine
                turned_im = odd_im * cosine - odd_re * sine
            out[k] = (even_re + turned_re, even_im + turned_im)
            out[count // 2 - k] = (even_re - turned_re, turned_im - even_im)
    return out


def fold_strip(radix, field, rows, fold_high, fold_low):
    nz = field.shape[1]
    length = nz // radix
    padded = -(-length // LANES) * LANES
    for piece in range(padded // LANES):
        blocks = []
        for block in range(radix):
            start = block * length + piece * LANES
            offset = start % LANES
            base = start - offset
            if offset == 0:
                blocks.append(field[rows, base : base + LANES])
            else:
                stop = min(base + 2 * LANES, nz)
                blocks.append(pltpu.roll(field[rows, base:stop], stop - base - offset, 1)[:, :LANES])
        waves = real_dft(blocks)
        for number, pair in enumerate(class_pairs(radix)):
            parts = (waves[0][0], waves[radix // 2][0]) if number == 0 else waves[pair[0]]
            for part in range(2):
                high, low = split(parts[part])
                columns = slice(part * padded + piece * LANES, part * padded + (piece + 1) * LANES)
                fold_high[number, rows, columns] = high
                fold_low[number, rows, columns] = low


def plane_kernel(radix, plane, places, plane_slot, field, table, axial, shift, sent, kept, *scratch):
    velocity, span, wave, turn, fold_high, fold_low, y, total, load_done, rest_done, out_done = scratch
    planes, rows, _ = field.shape
    half_count, count, _ = sent.shape
    shares = 2 * half_count
    me = lax.axis_index("pencil")
    first_plane = lax.axis_index("plane") * planes
    slot = plane_slot[first_plane + plane] - first_plane
    strip = 16
    cut = rows // load_done.shape[0]
    loads = []
    for piece in range(rows // cut):
        part = pl.ds(piece * cut, cut)
        loads.append(pltpu.make_async_copy(field.at[slot, part], velocity.at[part], load_done.at[piece]))
    rest = [
        pltpu.make_async_copy(source, target, rest_done.at[index])
        for index, (source, target) in enumerate(((table, span), (shift.at[me], turn), (axial.at[me], wave)))
    ]
    loads[0].start()
    for copy in rest:
        copy.start()
    for copy in loads[1:]:
        copy.start()
    for piece in range(rows // cut):
        loads[piece].wait()

        def fold(index, carry):
            first = pl.multiple_of(piece * cut + index * strip, strip)
            fold_strip(radix, velocity, pl.ds(first, strip), fold_high, fold_low)
            return carry

        lax.fori_loop(0, cut // strip, fold, 0, unroll=2)
    rest[0].wait()
    rest[1].wait()
    cos_shift = turn[0:1, :]
    sin_shift = turn[1:2, :]
    half = shares * 2 * GROUP
    for number in range(radix // 2):
        both = dot_nt(span[number], fold_high[number])
        value = both[: 2 * half] + both[2 * half :] + dot_nt(span[number, : 2 * half], fold_low[number])
        re_part = value[:half]
        im_part = value[half:]
        turned = (
            re_part * cos_shift - im_part * sin_shift,
            re_part * sin_shift + im_part * cos_shift,
        )
        for part in range(2):
            high, low = split(turned[part])
            first = (number * 2 + part) * 2 * GROUP
            for owner in range(shares):
                place = places[me * shares + owner]
                owned = slice(owner * 2 * GROUP, (owner + 1) * 2 * GROUP)
                y[place, first : first + 2 * GROUP, :rows] = high[owned]
                y[place, first : first + 2 * GROUP, rows:] = low[owned]
    rest[2].wait()
    owners = 2 if half_count % 2 == 0 else 1
    leaving = []
    for first in range(0, shares, owners):
        left = y[first : first + owners].reshape(owners * count, 2 * rows)
        value = dot_nn(left, wave[: 2 * rows]) + dot_nn(left[:, :rows], wave[2 * rows :])
        window = pl.ds(first, owners)
        total[window] = value.reshape(owners, count, KX)
        target = sent.at[window] if first < half_count else kept.at[pl.ds(first - half_count, owners)]
        leaving.append(pltpu.make_async_copy(total.at[window], target, out_done.at[first // owners]))
        leaving[-1].start()
    for copy in leaving:
        copy.wait()


def transform_plane(plane, places, plane_slot, field, table, axial, shift, radix):
    planes, rows, nz = field.shape
    shares = axial.shape[0]
    half_count = shares // 2
    pairs, table_rows, depth = table.shape
    count = pairs * 4 * GROUP
    out = jax.ShapeDtypeStruct((half_count, count, KX), F32)
    pieces = rows // LANES if rows % LANES == 0 else 1
    smem = pl.BlockSpec(memory_space=pltpu.SMEM)
    hbm = pl.BlockSpec(memory_space=pl.ANY)
    return pl.pallas_call(
        functools.partial(plane_kernel, radix, plane),
        out_shape=(out, out),
        in_specs=[smem, smem, hbm, hbm, hbm, hbm],
        out_specs=(hbm, hbm),
        scratch_shapes=[
            pltpu.VMEM((rows, nz), F32),
            pltpu.VMEM(table.shape, BF16),
            pltpu.VMEM(axial.shape[1:], BF16),
            pltpu.VMEM(shift.shape[1:], F32),
            pltpu.VMEM((pairs, rows, depth), BF16),
            pltpu.VMEM((pairs, rows, depth), BF16),
            pltpu.VMEM((shares, count, 2 * rows), BF16),
            pltpu.VMEM((shares, count, KX), F32),
            pltpu.SemaphoreType.DMA((pieces,)),
            pltpu.SemaphoreType.DMA((3,)),
            pltpu.SemaphoreType.DMA((shares,)),
        ],
        compiler_params=pltpu.CompilerParams(vmem_limit_bytes=56 * 1024 * 1024),
        cost_estimate=pl.CostEstimate(
            flops=3 * rows * pairs * table_rows * depth + 6 * shares * count * rows * KX,
            bytes_accessed=rows * nz * 4 + pairs * table_rows * depth * 2 + shares * count * KX * 4,
            transcendentals=0,
        ),
        name="plane",
    )(places, plane_slot, field, table, axial, shift)


def cross_kernel(radix, planes, offsets, band_slots, partner_slots, pairs, *refs):
    sources = dict(zip(offsets, refs[: len(offsets)]))
    band_out, partner_out, wanted, woven = refs[-4:]
    band = wanted.shape[0] // (2 * planes)
    share = woven.shape[2]
    side = pl.program_id(1)

    @pl.when((pl.program_id(0) == 0) & (side == 0))
    def _():
        first_plane = lax.axis_index("plane") * planes

        def clear(index, carry):
            wanted[index] = 0
            return carry

        lax.fori_loop(0, 2 * planes * band, clear, 0)

        def mark(index, carry):
            lower = pairs[index, 0]
            upper = pairs[index, 1]
            for end, plane in enumerate((lower - first_plane, upper - first_plane)):

                @pl.when((plane >= 0) & (plane < planes))
                def _():
                    wanted[(end * planes + plane) * band + upper - lower] = 1

            return carry

        lax.fori_loop(0, pairs.shape[0], mark, 0)

    residues = [residue for pair in class_pairs(radix) for residue in pair]

    def parts(source):
        value = source[0].reshape(radix // 2, 2, 2 * GROUP, 2 * LANES)
        re_rows = value[:, 0].reshape(share, 2 * LANES)
        im_rows = value[:, 1].reshape(share, 2 * LANES)
        return re_rows[:, :LANES], re_rows[:, LANES:], im_rows[:, :LANES], im_rows[:, LANES:]

    def weave(index, values):
        for part in range(2):
            for number, residue in enumerate(residues):
                woven[index, part, pl.ds(residue, GROUP, stride=radix), :] = values[part][
                    number * GROUP : (number + 1) * GROUP
                ]

    @pl.when(side == 0)
    def _():
        for index, offset in enumerate(offsets):
            re_cos, re_sin, im_cos, im_sin = parts(sources[offset])
            weave(index, (re_cos + im_sin, im_cos - re_sin))

    @pl.when(side == 1)
    def _():
        row = lax.broadcasted_iota(jnp.int32, (LANES, LANES), 0)
        column = lax.broadcasted_iota(jnp.int32, (LANES, LANES), 1)
        mirror = (row + column == LANES - 1).astype(BF16)

        def mirrored(value):
            high = value.astype(BF16)
            middle, low = split(value - high.astype(F32))
            return dot_nn(high, mirror) + dot_nn(middle, mirror) + dot_nn(low, mirror)

        for index, offset in enumerate(offsets):
            re_cos, re_sin, im_cos, im_sin = parts(sources[offset])
            weave(index, (mirrored(re_cos - im_sin), mirrored(im_cos + re_sin)))

    def spectrum(offset):
        index = offsets.index(offset)
        return woven[index, 0], woven[index, 1]

    for out, slots, end in ((band_out, band_slots, 0), (partner_out, partner_slots, 1)):
        for place, own, gap in slots:
            keep = wanted[(end * planes + own) * band + gap] != 0
            own_re, own_im = spectrum(own)
            if end == 0:
                far_re, far_im = spectrum(own + gap)
                imag = own_im * far_re - own_re * far_im
            else:
                far_re, far_im = spectrum(own - gap)
                imag = far_re * own_im - far_im * own_re
            out[place + (0,)] = jnp.where(keep, own_re * far_re + own_im * far_im, 0.0)
            out[place + (1,)] = jnp.where(keep, imag, 0.0)


def cross(pairs, sources, earlier, planes, band, radix, last):
    share = radix * GROUP
    blocks = KX // 2 // LANES
    out = jax.ShapeDtypeStruct((planes, band, 2, share, KX), F32)

    def lane_block(block, side):
        return block + side * (2 * blocks - 1 - 2 * block)

    slots = {0: [], 1: []}
    if last:
        places = {0: (planes - 1, band - 1), 1: (0, band - 1)}
        slots = {0: [((0, 0), planes - 1, band - 1)], 1: [((0, 0), 0, band - 1)]}
        out_specs = tuple(
            pl.BlockSpec(
                (1, 1, 2, share, LANES),
                functools.partial(lambda end, b, side: places[end] + (0, 0, lane_block(b, side)), end),
            )
            for end in range(2)
        )
    else:
        for own in range(planes):
            for gap in range(band):
                for end in range(2):
                    far = own + gap if end == 0 else own - gap
                    if far in sources:
                        slots[end].append(((own, gap), own, gap))
        spec = pl.BlockSpec(
            (planes, band, 2, share, LANES), lambda b, side: (0, 0, 0, 0, lane_block(b, side))
        )
        out_specs = (spec, spec)
    used = sorted(
        {own for end in range(2) for _, own, _ in slots[end]}
        | {own + gap for _, own, gap in slots[0]}
        | {own - gap for _, own, gap in slots[1]}
    )
    specs = [pl.BlockSpec(memory_space=pltpu.SMEM)]
    specs += [pl.BlockSpec((1, 2 * share, 2 * LANES), lambda b, side: (0, 0, b))] * len(used)
    specs += [pl.BlockSpec(memory_space=pl.ANY)] * len(earlier)
    return pl.pallas_call(
        functools.partial(cross_kernel, radix, planes, used, slots[0], slots[1]),
        out_shape=(out, out),
        grid=(blocks, 2),
        in_specs=specs,
        out_specs=out_specs,
        scratch_shapes=[
            pltpu.SMEM((2 * planes * band,), jnp.int32),
            pltpu.VMEM((len(used), 2, share, LANES), F32),
        ],
        input_output_aliases={1 + len(used) + i: i for i in range(len(earlier))},
        compiler_params=pltpu.CompilerParams(vmem_limit_bytes=48 * 1024 * 1024),
        cost_estimate=pl.CostEstimate(
            flops=(len(slots[0]) + len(slots[1])) * share * KX * 6 + len(used) * share * KX * 200,
            bytes_accessed=(len(slots[0]) + len(slots[1]) + len(used)) * share * KX * 8,
            transcendentals=0,
        ),
        name="cross",
    )(pairs, *[sources[offset] for offset in used], *earlier)


def solution(mesh):
    shares = mesh.shape["pencil"]
    slabs = mesh.shape["plane"]
    reach = slabs // 2
    orders = halving_orders(shares)
    radix = KZ // shares // GROUP
    core_swap = [(i, i ^ 1) for i in range(shares)]
    swaps = [
        [(i, i ^ (1 << orders[i & 1][step])) for i in range(shares)] for step in range(len(orders[0]))
    ]
    upward = [(i, i + 1) for i in range(slabs - 1)]
    downward = [(i + 1, i) for i in range(slabs - 1)]

    def local(velocity, plane_slot, pair_list):
        planes, rows, nz = velocity.shape
        band = planes * reach
        table = span_table(nz, shares, radix)
        axial = axial_table(rows * shares, nz, shares)
        shift = shift_table(rows * shares, shares)
        places = place_table(shares).reshape(-1)

        def after(value, *earlier):
            return lax.optimization_barrier((value,) + earlier)[0]

        near, far = {}, {}
        gates = {}
        for plane in range(planes):
            sent, kept = transform_plane(
                plane, places, plane_slot, velocity, table, axial, shift, radix
            )
            terms = [kept, lax.ppermute(sent, "pencil", core_swap)]
            count = shares // 2
            first_hops = []
            for step, swap in enumerate(swaps):
                count //= 2
                leaving = functools.reduce(lambda a, b: a + b, [term[count : 2 * count] for term in terms])
                if plane:
                    leaving = after(leaving, *gates["sum" if step == 0 else "hop"])
                if step == 0:
                    gates["core"] = leaving
                terms.append(lax.ppermute(leaving, "pencil", swap))
                if step == 0:
                    gates["sum"] = [terms[-1]]
            near[plane] = functools.reduce(lambda a, b: a + b, [term[:1] for term in terms])
            below, above = near[plane], near[plane]
            for away in range(1, reach + 1):
                home = near if away < reach else far
                if away < reach or plane > 0:
                    if away == reach and far:
                        below = after(below, *far.values())
                    below = lax.ppermute(below, "plane", upward)
                    home[plane - away * planes] = below
                    first_hops.append(below)
                if away < reach or plane < planes - 1:
                    above = lax.ppermute(above, "plane", downward)
                    home[plane + away * planes] = above
                    first_hops.append(above)
            gates["hop"] = first_hops[:2]
        outputs = cross(pair_list, near, (), planes, band, radix, False)
        return tuple(cross(pair_list, {**near, **far}, outputs, planes, band, radix, True))

    return jax.shard_map(
        local,
        mesh=mesh,
        in_specs=(P("plane", "pencil", None), P(), P()),
        out_specs=(P("plane", None, None, "pencil", None), P("plane", None, None, "pencil", None)),
        check_vma=False,
    )
```

time: 817 us -> 130 us (0.16)
  matrix products: 515 us -> 0 us
  waiting for transfers between devices: 197 us -> 45 us
  local copies, waits for them, and re-layouts: 62.5 us -> 0.11 us
  Pallas kernels: 0 us -> 53.8 us
  starting transfers between devices: 5.55 us -> 28.4 us
  other arithmetic: 16.6 us -> 1.14 us
  between operations: 14.7 us -> 0.75 us
    dot_general x8 -> x0, matrix products: 515 us -> none  [the longest x4 390 us: local(): jnp.dot(flat_field, spanwise_table(first_col, col_block, mode_share), pre...]
    all_to_all x1 -> x0, waiting for transfers between devices: 117 us -> none  [local(): lax.all_to_all(halfway, 'pencil', split_axis=2, concat_axis=1, tiled=True)]
    all_gather x1 -> x0, waiting for transfers between devices: 80.2 us -> none  [local(): everything = lax.all_gather(spectra, 'plane', axis=0, tiled=True)]
    pallas_call x0 -> x4, Pallas kernels: none -> 53.8 us  [the longest x2 43.8 us: transform_plane(): pl.pallas_call(functools.partial(plane_kernel, radix, plane), out_shape=(...]
    ppermute x0 -> x12, waiting for transfers between devices: none -> 45 us  [the longest x4 29.3 us: local(): terms.append(lax.ppermute(leaving, 'pencil', swap))]
    ppermute x0 -> x12, starting transfers between devices: none -> 28.4 us  [the longest x3 14.7 us: local(): below = lax.ppermute(below, 'plane', upward)]
    all_to_all x2 -> x0, local copies, waits for them, and re-layouts: 25.9 us -> none  [local(): lax.all_to_all(halfway, 'pencil', split_axis=2, concat_axis=1, tiled=True)]
    reshape x2 -> x0, local copies, waits for them, and re-layouts: 16.4 us -> none  [the longest x1 13.1 us: local(): halfway = jnp.concatenate(pieces, axis=1).reshape(planes, row_count, 2 * KZ)]
  transfers between devices with their start and end apart: 2 -> 12, of which waited for: 2 -> 8; matrix products, arithmetic and copies ran while one was open for 0% -> 1% of each run, Pallas kernels for 0% -> 22%
where the time goes in v2:
time: 130 us; the launch traced here: 129 us
  Pallas kernels  53.8 us (41%)
  waiting for transfers between devices  45 us (35%)
  starting transfers between devices  28.4 us (22%)
    pallas_call x2, Pallas kernels, transform_plane(): pl.pallas_call(functools.partial(plane_kernel, radix, plane), out_shape=(...  43.8 us
    ppermute x4, waiting for transfers between devices, local(): terms.append(lax.ppermute(leaving, 'pencil', swap))  29.3 us
    ppermute x3, starting transfers between devices, local(): below = lax.ppermute(below, 'plane', upward)  14.7 us
    ppermute x3, waiting for transfers between devices, local(): below = lax.ppermute(below, 'plane', upward)  10.5 us
    pallas_call x2, Pallas kernels, cross(): pl.pallas_call(functools.partial(cross_kernel, radix, planes, used, slots...  10 us
    ppermute x4, starting transfers between devices, local(): terms.append(lax.ppermute(leaving, 'pencil', swap))  9.26 us
    ppermute x3, waiting for transfers between devices, local(): above = lax.ppermute(above, 'plane', downward)  5.21 us
    ppermute x3, starting transfers between devices, local(): above = lax.ppermute(above, 'plane', downward)  3.85 us
  transfers between devices with their start and end apart: 12, of which 8 were waited for; matrix products, arithmetic and copies ran while one was open for 1% of the time, Pallas kernels for 22%

profile of v2, /device:TPU:0, one launch (start us, length us, event | category | flops | bytes accessed | tf_op | source)
XLA Modules:
  0.0 129.2 jit_solution(3344238729561611808)
XLA Ops:
  0.6 21.8 %plane.3 = (f32[4,256,512]{2,1,0:T(8,128)}, f32[4,256,512]{2,1,0:T(8,128)}) custom-call(s32[64]{0:T(128)} %constant.8.clone.places, s32[8]{0:T(128)} %plane_slot.3, f32[2,640,3840]{2,1,0:T(8,128)} %field.3, bf16[8,512,512]{2,1,0:T(8,128)(2,1)} %constant.9.clone.table, bf16[8,1920,512]{2,1,0:T(8,128)(2,1)} %constant.10.clone.axial, ...), custom_call_target="tpu_custom_call" | custom-call | flops 8053063680 | bytes 18219008 | tf_op jit(solution)/shard_map/plane/pallas_call | solution.py:244
  22.4 0.5 collective-permute-start.1
  22.9 22.0 %plane.2 = (f32[4,256,512]{2,1,0:T(8,128)}, f32[4,256,512]{2,1,0:T(8,128)}) custom-call(s32[64]{0:T(128)} %constant.8.clone.places, s32[8]{0:T(128)} %plane_slot.3, f32[2,640,3840]{2,1,0:T(8,128)} %field.3, bf16[8,512,512]{2,1,0:T(8,128)(2,1)} %constant.9.clone.table, bf16[8,1920,512]{2,1,0:T(8,128)(2,1)} %constant.10.clone.axial, ...), custom_call_target="tpu_custom_call" | custom-call | flops 8053063680 | bytes 18219008 | tf_op jit(solution)/shard_map/plane/pallas_call | solution.py:244
  45.0 0.1 collective-permute-start
  45.1 0.2 slice_add_fusion
  45.3 2.9 %collective-permute-start.2 = (f32[2,256,512]{2,1,0:T(8,128)S(1)}, f32[2,256,512]{2,1,0:T(8,128)S(1)}, u32[]{:S(2)}, u32[]{:S(2)}) collective-permute-start(f32[2,256,512]{2,1,0:T(8,128)S(1)} %slice_add_fusion), channel_id=1, source_target_pairs={{0,2},{1,5},{2,0},{3,7},{4,6},{5,1},{6,4},{7,3},{8,10},{9,13},{10,... | collective-permute-start | bytes 3145736 | tf_op jit(solution)/shard_map/ppermute | solution.py:455
  48.2 12.8 %collective-permute-done.2 = f32[2,256,512]{2,1,0:T(8,128)S(1)} collective-permute-done((f32[2,256,512]{2,1,0:T(8,128)S(1)}, f32[2,256,512]{2,1,0:T(8,128)S(1)}, u32[]{:S(2)}, u32[]{:S(2)}) %collective-permute-start.2) | collective-permute-done | bytes 1048608 | tf_op jit(solution)/shard_map/ppermute | solution.py:455
  61.0 0.1 slice_add_fusion.2
  61.1 2.1 %collective-permute-start.4 = (f32[1,256,512]{2,1,0:T(8,128)S(1)}, f32[1,256,512]{2,1,0:T(8,128)S(1)}, u32[]{:S(2)}, u32[]{:S(2)}) collective-permute-start(f32[1,256,512]{2,1,0:T(8,128)S(1)} %slice_add_fusion.2), channel_id=1, source_target_pairs={{0,4},{1,3},{2,6},{3,1},{4,0},{5,7},{6,2},{7,5},{8,12},{9,11},{10,... | collective-permute-start | bytes 1572872 | tf_op jit(solution)/shard_map/ppermute | solution.py:455
  63.2 0.2 slice_add_fusion.1
  63.4 1.6 %collective-permute-start.3 = (f32[2,256,512]{2,1,0:T(8,128)S(1)}, f32[2,256,512]{2,1,0:T(8,128)S(1)}, u32[]{:S(2)}, u32[]{:S(2)}) collective-permute-start(f32[2,256,512]{2,1,0:T(8,128)S(1)} %slice_add_fusion.1), channel_id=1, source_target_pairs={{0,2},{1,5},{2,0},{3,7},{4,6},{5,1},{6,4},{7,3},{8,10},{9,13},{10,... | collective-permute-start | bytes 3145736 | tf_op jit(solution)/shard_map/ppermute | solution.py:455
  65.0 10.7 %collective-permute-done.4 = f32[1,256,512]{2,1,0:T(8,128)S(1)} collective-permute-done((f32[1,256,512]{2,1,0:T(8,128)S(1)}, f32[1,256,512]{2,1,0:T(8,128)S(1)}, u32[]{:S(2)}, u32[]{:S(2)}) %collective-permute-start.4) | collective-permute-done | bytes 524320 | tf_op jit(solution)/shard_map/ppermute | solution.py:455
  75.7 0.2 fusion.refs_2_.refs_1_
  75.9 0.0 copy-start.2
  75.9 1.3 collective-permute-start.6
  77.2 5.0 %collective-permute-start.5 = (f32[1,256,512]{2,1,0:T(8,128)S(1)}, f32[1,256,512]{2,1,0:T(8,128)S(1)}, u32[]{:S(2)}, u32[]{:S(2)}) collective-permute-start(f32[1,256,512]{2,1,0:T(8,128)S(1)} %fusion.refs_2_.refs_1_), channel_id=1, source_target_pairs={{0,8},{8,16},{16,24},{1,9},{9,17},{17,25},{2,10},{10,18},{18,26},{... | collective-permute-start | bytes 1572872 | tf_op jit(solution)/shard_map/ppermute | solution.py:465
  82.2 0.1 slice_add_fusion.6
  82.3 5.0 %collective-permute-done.6.refs_4_ = f32[1,256,512]{2,1,0:T(8,128)S(1)} collective-permute-done((f32[1,256,512]{2,1,0:T(8,128)S(1)}, f32[1,256,512]{2,1,0:T(8,128)S(1)}, u32[]{:S(2)}, u32[]{:S(2)}) %collective-permute-start.6) | collective-permute-done | bytes 524320 | tf_op jit(solution)/shard_map/ppermute | solution.py:469
  87.4 1.5 %collective-permute-done.5.refs_0_ = f32[1,256,512]{2,1,0:T(8,128)S(1)} collective-permute-done((f32[1,256,512]{2,1,0:T(8,128)S(1)}, f32[1,256,512]{2,1,0:T(8,128)S(1)}, u32[]{:S(2)}, u32[]{:S(2)}) %collective-permute-start.5) | collective-permute-done | bytes 524320 | tf_op jit(solution)/shard_map/ppermute | solution.py:465
  88.8 2.7 %collective-permute-start.7 = (f32[1,256,512]{2,1,0:T(8,128)S(1)}, f32[1,256,512]{2,1,0:T(8,128)S(1)}, u32[]{:S(2)}, u32[]{:S(2)}) collective-permute-start(f32[1,256,512]{2,1,0:T(8,128)S(1)} %slice_add_fusion.6), channel_id=1, source_target_pairs={{0,4},{1,3},{2,6},{3,1},{4,0},{5,7},{6,2},{7,5},{8,12},{9,11},{10,... | collective-permute-start | bytes 1572872 | tf_op jit(solution)/shard_map/ppermute | solution.py:455
  91.5 1.3 collective-permute-start.9
  92.8 5.9 %collective-permute-done.7 = f32[1,256,512]{2,1,0:T(8,128)S(1)} collective-permute-done((f32[1,256,512]{2,1,0:T(8,128)S(1)}, f32[1,256,512]{2,1,0:T(8,128)S(1)}, u32[]{:S(2)}, u32[]{:S(2)}) %collective-permute-start.7) | collective-permute-done | bytes 524320 | tf_op jit(solution)/shard_map/ppermute | solution.py:455
  98.7 0.2 fusion.1.refs_3_.refs_2_
  98.9 5.2 %collective-permute-start.8 = (f32[1,256,512]{2,1,0:T(8,128)S(1)}, f32[1,256,512]{2,1,0:T(8,128)}, u32[]{:S(2)}, u32[]{:S(2)}) collective-permute-start(f32[1,256,512]{2,1,0:T(8,128)S(1)} %fusion.1.refs_3_.refs_2_), channel_id=1, source_target_pairs={{0,8},{8,16},{16,24},{1,9},{9,17},{17,25},{2,10},{10,18},{18,26},{... | collective-permute-start | bytes 1572872 | tf_op jit(solution)/shard_map/ppermute | solution.py:465
  104.1 1.3 collective-permute-start.11
  105.4 0.2 collective-permute-done.9.refs_3_
  105.6 8.3 %collective-permute-done.8.refs_1_ = f32[1,256,512]{2,1,0:T(8,128)} collective-permute-done((f32[1,256,512]{2,1,0:T(8,128)S(1)}, f32[1,256,512]{2,1,0:T(8,128)}, u32[]{:S(2)}, u32[]{:S(2)}) %collective-permute-start.8) | collective-permute-done | bytes 524320 | tf_op jit(solution)/shard_map/ppermute | solution.py:465
  113.9 4.5 %collective-permute-start.10 = (f32[1,256,512]{2,1,0:T(8,128)}, f32[1,256,512]{2,1,0:T(8,128)S(1)}, u32[]{:S(2)}, u32[]{:S(2)}) collective-permute-start(f32[1,256,512]{2,1,0:T(8,128)} %collective-permute-done.8.refs_1_), channel_id=1, source_target_pairs={{0,8},{8,16},{16,24},{1,9},{9,17},{17,25},{2,10},{10,18},{18,26},{... | collective-permute-start | bytes 1572872 | tf_op jit(solution)/shard_map/ppermute | solution.py:465
  118.4 0.1 copy.12.pairs
  118.5 6.2 %cross.2 = (f32[2,4,2,128,512]{4,3,2,1,0:T(8,128)}, f32[2,4,2,128,512]{4,3,2,1,0:T(8,128)}) custom-call(s32[20,2]{1,0:T(8,128)S(1)} %copy.12.pairs, f32[1,256,512]{2,1,0:T(8,128)S(1)} %collective-permute-done.5.refs_0_, f32[1,256,512]{2,1,0:T(8,128)} %collective-permute-done.8.refs_1_, f32[1,256,512]{2,1,0:T(8,128)S(1)} %fusion.refs_2_.refs_1_, ...), custom_call_target="tpu_custom_call" | custom-call | flops 84148224 | bytes 10485760 | tf_op jit(solution)/shard_map/cross/pallas_call | solution.py:394
  124.7 0.7 collective-permute-done.10.refs_0_
  125.4 3.9 %cross.3 = (f32[2,4,2,128,512]{4,3,2,1,0:T(8,128)}, f32[2,4,2,128,512]{4,3,2,1,0:T(8,128)}) custom-call(s32[20,2]{1,0:T(8,128)S(1)} %copy.12.pairs, f32[1,256,512]{2,1,0:T(8,128)S(1)} %collective-permute-done.10.refs_0_, f32[1,256,512]{2,1,0:T(8,128)S(1)} %fusion.refs_2_.refs_1_, ...), custom_call_target="tpu_custom_call", output_to_operand_aliasing={{0}: (5, {}), {1}: (6, {})} | custom-call | flops 53215232 | bytes 3145728 | tf_op jit(solution)/shard_map/cross/pallas_call | solution.py:394
  (9 shorter events, 0.0 us)
Async XLA Ops:
  22.4 22.7 %copy-start.1 = (f32[4,256,512]{2,1,0:T(8,128)S(1)}, f32[4,256,512]{2,1,0:T(8,128)}, u32[]{:S(2)}) copy-start(f32[4,256,512]{2,1,0:T(8,128)} %get-tuple-element.13) | copy-start | bytes 6291460
  22.4 22.7 %collective-permute-start.1 = (f32[4,256,512]{2,1,0:T(8,128)}, f32[4,256,512]{2,1,0:T(8,128)S(1)}, u32[]{:S(2)}, u32[]{:S(2)}) collective-permute-start(f32[4,256,512]{2,1,0:T(8,128)} %get-tuple-element.14), channel_id=1, source_target_pairs={{0,1},{1,0},{2,3},{3,2},{4,5},{5,4},{6,7},{7,6},{8,9},{9,8},{10,11... | collective-permute-start | bytes 6291464 | tf_op jit(solution)/shard_map/ppermute | solution.py:445
  45.0 18.3 %collective-permute-start = (f32[4,256,512]{2,1,0:T(8,128)}, f32[4,256,512]{2,1,0:T(8,128)S(1)}, u32[]{:S(2)}, u32[]{:S(2)}) collective-permute-start(f32[4,256,512]{2,1,0:T(8,128)} %get-tuple-element.12), channel_id=1, source_target_pairs={{0,1},{1,0},{2,3},{3,2},{4,5},{5,4},{6,7},{7,6},{8,9},{9,8},{10,11... | collective-permute-start | bytes 6291464 | tf_op jit(solution)/shard_map/ppermute | solution.py:445
  45.1 18.1 %copy-start = (f32[4,256,512]{2,1,0:T(8,128)S(1)}, f32[4,256,512]{2,1,0:T(8,128)}, u32[]{:S(2)}) copy-start(f32[4,256,512]{2,1,0:T(8,128)} %get-tuple-element.11) | copy-start | bytes 6291460
  45.3 15.6 %collective-permute-start.2 = (f32[2,256,512]{2,1,0:T(8,128)S(1)}, f32[2,256,512]{2,1,0:T(8,128)S(1)}, u32[]{:S(2)}, u32[]{:S(2)}) collective-permute-start(f32[2,256,512]{2,1,0:T(8,128)S(1)} %slice_add_fusion), channel_id=1, source_target_pairs={{0,2},{1,5},{2,0},{3,7},{4,6},{5,1},{6,4},{7,3},{8,10},{9,13},{10,... | collective-permute-start | bytes 3145736 | tf_op jit(solution)/shard_map/ppermute | solution.py:455
  61.1 14.6 %collective-permute-start.4 = (f32[1,256,512]{2,1,0:T(8,128)S(1)}, f32[1,256,512]{2,1,0:T(8,128)S(1)}, u32[]{:S(2)}, u32[]{:S(2)}) collective-permute-start(f32[1,256,512]{2,1,0:T(8,128)S(1)} %slice_add_fusion.2), channel_id=1, source_target_pairs={{0,4},{1,3},{2,6},{3,1},{4,0},{5,7},{6,2},{7,5},{8,12},{9,11},{10,... | collective-permute-start | bytes 1572872 | tf_op jit(solution)/shard_map/ppermute | solution.py:455
  63.4 18.7 %collective-permute-start.3 = (f32[2,256,512]{2,1,0:T(8,128)S(1)}, f32[2,256,512]{2,1,0:T(8,128)S(1)}, u32[]{:S(2)}, u32[]{:S(2)}) collective-permute-start(f32[2,256,512]{2,1,0:T(8,128)S(1)} %slice_add_fusion.1), channel_id=1, source_target_pairs={{0,2},{1,5},{2,0},{3,7},{4,6},{5,1},{6,4},{7,3},{8,10},{9,13},{10,... | collective-permute-start | bytes 3145736 | tf_op jit(solution)/shard_map/ppermute | solution.py:455
  75.9 42.5 %copy-start.2 = (s32[20,2]{0,1:T(2,128)S(1)}, s32[20,2]{0,1:T(2,128)}, u32[]{:S(2)}) copy-start(s32[20,2]{0,1:T(2,128)} %param.9) | copy-start | bytes 484
  75.9 11.5 %collective-permute-start.6 = (f32[1,256,512]{2,1,0:T(8,128)S(1)}, f32[1,256,512]{2,1,0:T(8,128)S(1)}, u32[]{:S(2)}, u32[]{:S(2)}) collective-permute-start(f32[1,256,512]{2,1,0:T(8,128)S(1)} %fusion.refs_2_.refs_1_), channel_id=1, source_target_pairs={{8,0},{16,8},{24,16},{9,1},{17,9},{25,17},{10,2},{18,10},{26,18},{... | collective-permute-start | bytes 1572872 | tf_op jit(solution)/shard_map/ppermute | solution.py:469
  77.2 11.6 %collective-permute-start.5 = (f32[1,256,512]{2,1,0:T(8,128)S(1)}, f32[1,256,512]{2,1,0:T(8,128)S(1)}, u32[]{:S(2)}, u32[]{:S(2)}) collective-permute-start(f32[1,256,512]{2,1,0:T(8,128)S(1)} %fusion.refs_2_.refs_1_), channel_id=1, source_target_pairs={{0,8},{8,16},{16,24},{1,9},{9,17},{17,25},{2,10},{10,18},{18,26},{... | collective-permute-start | bytes 1572872 | tf_op jit(solution)/shard_map/ppermute | solution.py:465
  88.8 9.9 %collective-permute-start.7 = (f32[1,256,512]{2,1,0:T(8,128)S(1)}, f32[1,256,512]{2,1,0:T(8,128)S(1)}, u32[]{:S(2)}, u32[]{:S(2)}) collective-permute-start(f32[1,256,512]{2,1,0:T(8,128)S(1)} %slice_add_fusion.6), channel_id=1, source_target_pairs={{0,4},{1,3},{2,6},{3,1},{4,0},{5,7},{6,2},{7,5},{8,12},{9,11},{10,... | collective-permute-start | bytes 1572872 | tf_op jit(solution)/shard_map/ppermute | solution.py:455
  91.5 14.0 %collective-permute-start.9 = (f32[1,256,512]{2,1,0:T(8,128)S(1)}, f32[1,256,512]{2,1,0:T(8,128)S(1)}, u32[]{:S(2)}, u32[]{:S(2)}) collective-permute-start(f32[1,256,512]{2,1,0:T(8,128)S(1)} %collective-permute-done.6.refs_4_), channel_id=1, source_target_pairs={{8,0},{16,8},{24,16},{9,1},{17,9},{25,17},{10,2},{18,10},{26,18},{... | collective-permute-start | bytes 1572872 | tf_op jit(solution)/shard_map/ppermute | solution.py:469
  98.9 15.0 %collective-permute-start.8 = (f32[1,256,512]{2,1,0:T(8,128)S(1)}, f32[1,256,512]{2,1,0:T(8,128)}, u32[]{:S(2)}, u32[]{:S(2)}) collective-permute-start(f32[1,256,512]{2,1,0:T(8,128)S(1)} %fusion.1.refs_3_.refs_2_), channel_id=1, source_target_pairs={{0,8},{8,16},{16,24},{1,9},{9,17},{17,25},{2,10},{10,18},{18,26},{... | collective-permute-start | bytes 1572872 | tf_op jit(solution)/shard_map/ppermute | solution.py:465
  104.1 14.4 %collective-permute-start.11 = (f32[1,256,512]{2,1,0:T(8,128)S(1)}, f32[1,256,512]{2,1,0:T(8,128)}, u32[]{:S(2)}, u32[]{:S(2)}) collective-permute-start(f32[1,256,512]{2,1,0:T(8,128)S(1)} %fusion.1.refs_3_.refs_2_), channel_id=1, source_target_pairs={{8,0},{16,8},{24,16},{9,1},{17,9},{25,17},{10,2},{18,10},{26,18},{... | collective-permute-start | bytes 1572872 | tf_op jit(solution)/shard_map/ppermute | solution.py:469
  113.9 11.5 %collective-permute-start.10 = (f32[1,256,512]{2,1,0:T(8,128)}, f32[1,256,512]{2,1,0:T(8,128)S(1)}, u32[]{:S(2)}, u32[]{:S(2)}) collective-permute-start(f32[1,256,512]{2,1,0:T(8,128)} %collective-permute-done.8.refs_1_), channel_id=1, source_target_pairs={{0,8},{8,16},{16,24},{1,9},{9,17},{17,25},{2,10},{10,18},{18,26},{... | collective-permute-start | bytes 1572872 | tf_op jit(solution)/shard_map/ppermute | solution.py:465

commit v3 on v2

--- a/solution.py
+++ b/solution.py
@@ -15,6 +15,7 @@
 KZ = 1024
 LANES = 128
 GROUP = 8
+VMEM_LIMIT = 56 * 1024 * 1024
 F32 = jnp.float32
 BF16 = jnp.bfloat16
 
@@ -162,11 +163,15 @@
                 fold_low[number, rows, columns] = low
 
 
-def plane_kernel(radix, plane, places, plane_slot, field, table, axial, shift, sent, kept, *scratch):
-    velocity, span, wave, turn, fold_high, fold_low, y, total, load_done, rest_done, out_done = scratch
+def start_all(copies):
+    for copy in copies:
+        copy.start()
+
+
+def span_phase(radix, plane, places, plane_slot, field, table, shift, y, scratch, after_pair):
+    velocity, span, turn, fold_high, fold_low, load_done, rest_done = scratch
     planes, rows, _ = field.shape
-    half_count, count, _ = sent.shape
-    shares = 2 * half_count
+    shares = y.shape[0]
     me = lax.axis_index("pencil")
     first_plane = lax.axis_index("plane") * planes
     slot = plane_slot[first_plane + plane] - first_plane
@@ -177,14 +182,12 @@
         part = pl.ds(piece * cut, cut)
         loads.append(pltpu.make_async_copy(field.at[slot, part], velocity.at[part], load_done.at[piece]))
     rest = [
-        pltpu.make_async_copy(source, target, rest_done.at[index])
-        for index, (source, target) in enumerate(((table, span), (shift.at[me], turn), (axial.at[me], wave)))
+        pltpu.make_async_copy(table, span, rest_done.at[0]),
+        pltpu.make_async_copy(shift.at[me], turn, rest_done.at[1]),
     ]
-    loads[0].start()
-    for copy in rest:
-        copy.start()
-    for copy in loads[1:]:
-        copy.start()
+    start_all(loads)
+    start_all(rest)
+    yield
     for piece in range(rows // cut):
         loads[piece].wait()
 
@@ -193,9 +196,9 @@
             fold_strip(radix, velocity, pl.ds(first, strip), fold_high, fold_low)
             return carry
 
-        lax.fori_loop(0, cut // strip, fold, 0, unroll=2)
-    rest[0].wait()
-    rest[1].wait()
+        lax.fori_loop(0, cut // strip, fold, 0, unroll=8 if cut % (8 * strip) == 0 else 2)
+    for copy in rest:
+        copy.wait()
     cos_shift = turn[0:1, :]
     sin_shift = turn[1:2, :]
     half = shares * 2 * GROUP
@@ -216,12 +219,20 @@
                 owned = slice(owner * 2 * GROUP, (owner + 1) * 2 * GROUP)
                 y[place, first : first + 2 * GROUP, :rows] = high[owned]
                 y[place, first : first + 2 * GROUP, rows:] = low[owned]
-    rest[2].wait()
-    owners = 2 if half_count % 2 == 0 else 1
+        after_pair(number)
+    yield
+
+
+def axial_phase(y, wave, total, sent, kept, out_done, before_group):
+    shares, count, width = y.shape
+    half_count = shares // 2
+    rows = width // 2
+    owners = shares // out_done.shape[0]
     leaving = []
     for first in range(0, shares, owners):
-        left = y[first : first + owners].reshape(owners * count, 2 * rows)
-        value = dot_nn(left, wave[: 2 * rows]) + dot_nn(left[:, :rows], wave[2 * rows :])
+        before_group(first // owners)
+        left = y[first : first + owners].reshape(owners * count, width)
+        value = dot_nn(left, wave[:width]) + dot_nn(left[:, :rows], wave[width:])
         window = pl.ds(first, owners)
         total[window] = value.reshape(owners, count, KX)
         target = sent.at[window] if first < half_count else kept.at[pl.ds(first - half_count, owners)]
@@ -231,42 +242,124 @@
         copy.wait()
 
 
-def transform_plane(plane, places, plane_slot, field, table, axial, shift, radix):
-    planes, rows, nz = field.shape
-    shares = axial.shape[0]
+def whole_kernel(radix, plane, places, plane_slot, field, table, shift, axial, sent, kept, y, wave, total, wave_done, out_done, *scratch):
+    phase = span_phase(radix, plane, places, plane_slot, field, table, shift, y, scratch, lambda number: None)
+    next(phase)
+    load = pltpu.make_async_copy(axial.at[lax.axis_index("pencil")], wave, wave_done)
+    load.start()
+    next(phase)
+    load.wait()
+    axial_phase(y, wave, total, sent, kept, out_done, lambda group: None)
+
+
+def span_kernel(radix, plane, places, plane_slot, field, table, shift, y_out, y, pair_done, *scratch):
+    height = y.shape[1] // (radix // 2)
+    copies = [
+        pltpu.make_async_copy(
+            y.at[:, pl.ds(number * height, height)], y_out.at[:, pl.ds(number * height, height)], pair_done.at[number]
+        )
+        for number in range(radix // 2)
+    ]
+    for _ in span_phase(
+        radix, plane, places, plane_slot, field, table, shift, y, scratch, lambda number: copies[number].start()
+    ):
+        pass
+    for copy in copies:
+        copy.wait()
+
+
+def axial_kernel(y_in, axial, sent, kept, y, wave, total, wave_done, out_done, in_done):
+    owners = y.shape[0] // out_done.shape[0]
+    load = pltpu.make_async_copy(axial.at[lax.axis_index("pencil")], wave, wave_done)
+    load.start()
+    copies = []
+    for group in range(out_done.shape[0]):
+        window = pl.ds(group * owners, owners)
+        copies.append(pltpu.make_async_copy(y_in.at[window], y.at[window], in_done.at[group]))
+    start_all(copies)
+    load.wait()
+    axial_phase(y, wave, total, sent, kept, out_done, lambda group: copies[group].wait())
+
+
+def transform_calls(planes, rows, nz, shares, radix):
+    table = span_table(nz, shares, radix)
+    axial = axial_table(rows * shares, nz, shares)
+    shift = shift_table(rows * shares, shares)
+    places = place_table(shares).reshape(-1)
     half_count = shares // 2
     pairs, table_rows, depth = table.shape
     count = pairs * 4 * GROUP
+    owners = 2 if half_count % 2 == 0 else 1
+    pieces = rows // LANES if rows % LANES == 0 else 1
     out = jax.ShapeDtypeStruct((half_count, count, KX), F32)
-    pieces = rows // LANES if rows % LANES == 0 else 1
+    modes = jax.ShapeDtypeStruct((shares, count, 2 * rows), BF16)
     smem = pl.BlockSpec(memory_space=pltpu.SMEM)
     hbm = pl.BlockSpec(memory_space=pl.ANY)
-    return pl.pallas_call(
-        functools.partial(plane_kernel, radix, plane),
-        out_shape=(out, out),
-        in_specs=[smem, smem, hbm, hbm, hbm, hbm],
-        out_specs=(hbm, hbm),
-        scratch_shapes=[
-            pltpu.VMEM((rows, nz), F32),
-            pltpu.VMEM(table.shape, BF16),
-            pltpu.VMEM(axial.shape[1:], BF16),
-            pltpu.VMEM(shift.shape[1:], F32),
-            pltpu.VMEM((pairs, rows, depth), BF16),
-            pltpu.VMEM((pairs, rows, depth), BF16),
-            pltpu.VMEM((shares, count, 2 * rows), BF16),
-            pltpu.VMEM((shares, count, KX), F32),
-            pltpu.SemaphoreType.DMA((pieces,)),
-            pltpu.SemaphoreType.DMA((3,)),
-            pltpu.SemaphoreType.DMA((shares,)),
-        ],
-        compiler_params=pltpu.CompilerParams(vmem_limit_bytes=56 * 1024 * 1024),
-        cost_estimate=pl.CostEstimate(
-            flops=3 * rows * pairs * table_rows * depth + 6 * shares * count * rows * KX,
-            bytes_accessed=rows * nz * 4 + pairs * table_rows * depth * 2 + shares * count * KX * 4,
-            transcendentals=0,
-        ),
-        name="plane",
-    )(places, plane_slot, field, table, axial, shift)
+    one, many = pltpu.SemaphoreType.DMA(()), lambda number: pltpu.SemaphoreType.DMA((number,))
+    y = pltpu.VMEM(modes.shape, BF16)
+    span_scratch = [
+        pltpu.VMEM((rows, nz), F32),
+        pltpu.VMEM(table.shape, BF16),
+        pltpu.VMEM(shift.shape[1:], F32),
+        pltpu.VMEM((pairs, rows, depth), BF16),
+        pltpu.VMEM((pairs, rows, depth), BF16),
+        many(pieces),
+        many(2),
+    ]
+    axial_scratch = [
+        pltpu.VMEM(axial.shape[1:], BF16),
+        pltpu.VMEM((shares, count, KX), F32),
+        one,
+        many(shares // owners),
+    ]
+    span_cost = (3 * rows * pairs * table_rows * depth, rows * nz * 4 + pairs * table_rows * depth * 2)
+    axial_cost = (6 * shares * count * rows * KX, shares * count * (KX + rows) * 4)
+
+    def call(kernel, name, costs, ins, outs, scratch):
+        return pl.pallas_call(
+            kernel,
+            out_shape=outs,
+            in_specs=ins,
+            out_specs=jax.tree.map(lambda _: hbm, outs),
+            scratch_shapes=scratch,
+            compiler_params=pltpu.CompilerParams(vmem_limit_bytes=VMEM_LIMIT),
+            cost_estimate=pl.CostEstimate(
+                flops=sum(cost[0] for cost in costs), bytes_accessed=sum(cost[1] for cost in costs), transcendentals=0
+            ),
+            name=name,
+        )
+
+    def whole(plane, plane_slot, field):
+        return call(
+            functools.partial(whole_kernel, radix, plane),
+            "whole",
+            [span_cost, axial_cost],
+            [smem, smem, hbm, hbm, hbm, hbm],
+            (out, out),
+            [y] + axial_scratch + span_scratch,
+        )(places, plane_slot, field, table, shift, axial)
+
+    def span(plane, plane_slot, field):
+        return call(
+            functools.partial(span_kernel, radix, plane),
+            "span",
+            [span_cost],
+            [smem, smem, hbm, hbm, hbm],
+            modes,
+            [y, many(pairs)] + span_scratch,
+        )(places, plane_slot, field, table, shift)
+
+    def along_x(spanned):
+        return call(
+            axial_kernel,
+            "axial",
+            [axial_cost],
+            [hbm, hbm],
+            (out, out),
+            [y] + axial_scratch + [many(shares // owners)],
+        )(spanned, axial)
+
+    return whole, span, along_x
 
 
 def cross_kernel(radix, planes, offsets, band_slots, partner_slots, pairs, *refs):
@@ -428,33 +521,29 @@
     def local(velocity, plane_slot, pair_list):
         planes, rows, nz = velocity.shape
         band = planes * reach
-        table = span_table(nz, shares, radix)
-        axial = axial_table(rows * shares, nz, shares)
-        shift = shift_table(rows * shares, shares)
-        places = place_table(shares).reshape(-1)
+        whole, span, along_x = transform_calls(planes, rows, nz, shares, radix)
 
         def after(value, *earlier):
             return lax.optimization_barrier((value,) + earlier)[0]
 
         near, far = {}, {}
-        gates = {}
+        first_hops, first_sum, last_sum = [], None, None
         for plane in range(planes):
-            sent, kept = transform_plane(
-                plane, places, plane_slot, velocity, table, axial, shift, radix
-            )
+            sent, kept = whole(plane, plane_slot, velocity)
+            if plane:
+                sent = after(sent, first_sum)
             terms = [kept, lax.ppermute(sent, "pencil", core_swap)]
             count = shares // 2
-            first_hops = []
             for step, swap in enumerate(swaps):
                 count //= 2
                 leaving = functools.reduce(lambda a, b: a + b, [term[count : 2 * count] for term in terms])
-                if plane:
-                    leaving = after(leaving, *gates["sum" if step == 0 else "hop"])
-                if step == 0:
-                    gates["core"] = leaving
+                if plane and step == 1:
+                    leaving = after(leaving, *first_hops)
                 terms.append(lax.ppermute(leaving, "pencil", swap))
                 if step == 0:
-                    gates["sum"] = [terms[-1]]
+                    first_sum = terms[-1]
+            last_sum = terms[-1]
+            first_hops = []
             near[plane] = functools.reduce(lambda a, b: a + b, [term[:1] for term in terms])
             below, above = near[plane], near[plane]
             for away in range(1, reach + 1):
@@ -469,7 +558,7 @@
                     above = lax.ppermute(above, "plane", downward)
                     home[plane + away * planes] = above
                     first_hops.append(above)
-            gates["hop"] = first_hops[:2]
+            first_hops = first_hops[:2]
         outputs = cross(pair_list, near, (), planes, band, radix, False)
         return tuple(cross(pair_list, {**near, **far}, outputs, planes, band, radix, True))
 

time: 130 us -> 114 us (0.88)
  waiting for transfers between devices: 45 us -> 34.1 us
  Pallas kernels: 53.8 us -> 50.8 us
  starting transfers between devices: 28.4 us -> 25.8 us
    ppermute x4, waiting for transfers between devices: 29.3 us -> 14.8 us  [local(): terms.append(lax.ppermute(leaving, 'pencil', swap))]
    ppermute x2, waiting for transfers between devices: 0.01 us -> 6.61 us  [local(): terms = [kept, lax.ppermute(sent, 'pencil', core_swap)]]
    ppermute x3, waiting for transfers between devices: 10.5 us -> 7.01 us  [local(): below = lax.ppermute(below, 'plane', upward)]
    pallas_call x2, Pallas kernels: 43.8 us -> 40.8 us  [whole(): call(functools.partial(whole_kernel, radix, plane), 'whole', [span_cost,...]
    ppermute x4, starting transfers between devices: 9.26 us -> 7.09 us  [local(): terms.append(lax.ppermute(leaving, 'pencil', swap))]
  transfers between devices with their start and end apart: 12 -> 12, of which waited for: 8 -> 10; matrix products, arithmetic and copies ran while one was open for 1% -> 1% of each run, Pallas kernels for 22% -> 23%
where the time goes in v3:
time: 114 us
  Pallas kernels  50.8 us (45%)
  waiting for transfers between devices  34.1 us (30%)
  starting transfers between devices  25.8 us (23%)
  other arithmetic  2.36 us (2%)
    pallas_call x2, Pallas kernels, whole(): call(functools.partial(whole_kernel, radix, plane), 'whole', [span_cost,...  40.8 us
    ppermute x4, waiting for transfers between devices, local(): terms.append(lax.ppermute(leaving, 'pencil', swap))  14.8 us
    ppermute x3, starting transfers between devices, local(): below = lax.ppermute(below, 'plane', upward)  14.3 us
    pallas_call x2, Pallas kernels, cross(): pl.pallas_call(functools.partial(cross_kernel, radix, planes, used, slots...  10 us
    ppermute x4, starting transfers between devices, local(): terms.append(lax.ppermute(leaving, 'pencil', swap))  7.09 us
    ppermute x3, waiting for transfers between devices, local(): below = lax.ppermute(below, 'plane', upward)  7.01 us
    ppermute x2, waiting for transfers between devices, local(): terms = [kept, lax.ppermute(sent, 'pencil', core_swap)]  6.61 us
    ppermute x3, waiting for transfers between devices, local(): above = lax.ppermute(above, 'plane', downward)  5.71 us
  transfers between devices with their start and end apart: 12, of which 10 were waited for; matrix products, arithmetic and copies ran while one was open for 1% of the time, Pallas kernels for 23%

profile of v3, /device:TPU:0, one launch (start us, length us, event | category | flops | bytes accessed | tf_op | source)
XLA Modules:
  0.0 114.0 jit_solution(3793402912963397025)
XLA Ops:
  0.6 20.3 %whole.3 = (f32[4,256,512]{2,1,0:T(8,128)}, f32[4,256,512]{2,1,0:T(8,128)}) custom-call(s32[64]{0:T(128)} %constant.8.clone.places, s32[8]{0:T(128)} %plane_slot.3, f32[2,640,3840]{2,1,0:T(8,128)} %field.3, bf16[8,512,512]{2,1,0:T(8,128)(2,1)} %constant.9.clone.table, f32[8,8,640]{2,1,0:T(8,128)} %constant.10.clone.shift, ...), custom_call_target="tpu_custom_call" | custom-call | flops 8053063680 | bytes 23461888 | tf_op jit(solution)/shard_map/whole/pallas_call | solution.py:333
  21.0 0.5 collective-permute-start
  21.5 4.0 %collective-permute-done = f32[4,256,512]{2,1,0:T(8,128)S(1)} collective-permute-done((f32[4,256,512]{2,1,0:T(8,128)}, f32[4,256,512]{2,1,0:T(8,128)S(1)}, u32[]{:S(2)}, u32[]{:S(2)}) %collective-permute-start) | collective-permute-done | bytes 2097184 | tf_op jit(solution)/shard_map/ppermute | solution.py:535
  25.5 1.4 %slice_add_fusion.1 = f32[2,256,512]{2,1,0:T(8,128)S(1)} fusion(f32[4,256,512]{2,1,0:T(8,128)S(1)} %collective-permute-done, f32[4,256,512]{2,1,0:T(8,128)} %get-tuple-element.13), kind=kLoop, calls=%fused_computation.1 | loop fusion | flops 262144 | bytes 3145728 | tf_op jit(solution)/shard_map/add | solution.py:539
  26.9 2.9 %collective-permute-start.1 = (f32[2,256,512]{2,1,0:T(8,128)S(1)}, f32[2,256,512]{2,1,0:T(8,128)S(1)}, u32[]{:S(2)}, u32[]{:S(2)}) collective-permute-start(f32[2,256,512]{2,1,0:T(8,128)S(1)} %slice_add_fusion.1), channel_id=1, source_target_pairs={{0,2},{1,5},{2,0},{3,7},{4,6},{5,1},{6,4},{7,3},{8,10},{9,13},{10,... | collective-permute-start | bytes 3145736 | tf_op jit(solution)/shard_map/ppermute | solution.py:542
  29.8 20.5 %whole.2 = (f32[4,256,512]{2,1,0:T(8,128)}, f32[4,256,512]{2,1,0:T(8,128)}) custom-call(s32[64]{0:T(128)} %constant.8.clone.places, s32[8]{0:T(128)} %plane_slot.3, f32[2,640,3840]{2,1,0:T(8,128)} %field.3, bf16[8,512,512]{2,1,0:T(8,128)(2,1)} %constant.9.clone.table, f32[8,8,640]{2,1,0:T(8,128)} %constant.10.clone.shift, ...), custom_call_target="tpu_custom_call" | custom-call | flops 8053063680 | bytes 23461888 | tf_op jit(solution)/shard_map/whole/pallas_call | solution.py:333
  50.4 0.1 slice_add_fusion.2
  50.6 1.6 %collective-permute-start.4 = (f32[1,256,512]{2,1,0:T(8,128)S(1)}, f32[1,256,512]{2,1,0:T(8,128)S(1)}, u32[]{:S(2)}, u32[]{:S(2)}) collective-permute-start(f32[1,256,512]{2,1,0:T(8,128)S(1)} %slice_add_fusion.2), channel_id=1, source_target_pairs={{0,4},{1,3},{2,6},{3,1},{4,0},{5,7},{6,2},{7,5},{8,12},{9,11},{10,... | collective-permute-start | bytes 1572872 | tf_op jit(solution)/shard_map/ppermute | solution.py:542
  52.2 2.6 %collective-permute-done.2 = f32[4,256,512]{2,1,0:T(8,128)S(1)} collective-permute-done((f32[4,256,512]{2,1,0:T(8,128)}, f32[4,256,512]{2,1,0:T(8,128)S(1)}, u32[]{:S(2)}, u32[]{:S(2)}) %collective-permute-start.2) | collective-permute-done | bytes 2097184 | tf_op jit(solution)/shard_map/ppermute | solution.py:535
  54.8 0.2 slice_add_fusion
  55.0 1.1 collective-permute-start.3
  56.1 5.7 %collective-permute-done.4 = f32[1,256,512]{2,1,0:T(8,128)S(1)} collective-permute-done((f32[1,256,512]{2,1,0:T(8,128)S(1)}, f32[1,256,512]{2,1,0:T(8,128)S(1)}, u32[]{:S(2)}, u32[]{:S(2)}) %collective-permute-start.4) | collective-permute-done | bytes 524320 | tf_op jit(solution)/shard_map/ppermute | solution.py:542
  61.8 0.2 fusion.refs_2_.refs_1_
  62.0 1.3 %collective-permute-start.6 = (f32[1,256,512]{2,1,0:T(8,128)S(1)}, f32[1,256,512]{2,1,0:T(8,128)S(1)}, u32[]{:S(2)}, u32[]{:S(2)}) collective-permute-start(f32[1,256,512]{2,1,0:T(8,128)S(1)} %fusion.refs_2_.refs_1_), channel_id=1, source_target_pairs={{8,0},{16,8},{24,16},{9,1},{17,9},{25,17},{10,2},{18,10},{26,18},{... | collective-permute-start | bytes 1572872 | tf_op jit(solution)/shard_map/ppermute | solution.py:558
  63.3 4.6 %collective-permute-start.5 = (f32[1,256,512]{2,1,0:T(8,128)S(1)}, f32[1,256,512]{2,1,0:T(8,128)S(1)}, u32[]{:S(2)}, u32[]{:S(2)}) collective-permute-start(f32[1,256,512]{2,1,0:T(8,128)S(1)} %fusion.refs_2_.refs_1_), channel_id=1, source_target_pairs={{0,8},{8,16},{16,24},{1,9},{9,17},{17,25},{2,10},{10,18},{18,26},{... | collective-permute-start | bytes 1572872 | tf_op jit(solution)/shard_map/ppermute | solution.py:554
  67.9 2.7 %collective-permute-done.3 = f32[2,256,512]{2,1,0:T(8,128)S(1)} collective-permute-done((f32[2,256,512]{2,1,0:T(8,128)S(1)}, f32[2,256,512]{2,1,0:T(8,128)S(1)}, u32[]{:S(2)}, u32[]{:S(2)}) %collective-permute-start.3) | collective-permute-done | bytes 1048608 | tf_op jit(solution)/shard_map/ppermute | solution.py:542
  70.6 0.1 slice_add_fusion.6
  70.7 5.3 %collective-permute-done.6.refs_4_ = f32[1,256,512]{2,1,0:T(8,128)S(1)} collective-permute-done((f32[1,256,512]{2,1,0:T(8,128)S(1)}, f32[1,256,512]{2,1,0:T(8,128)S(1)}, u32[]{:S(2)}, u32[]{:S(2)}) %collective-permute-start.6) | collective-permute-done | bytes 524320 | tf_op jit(solution)/shard_map/ppermute | solution.py:558
  76.1 1.2 %collective-permute-done.5.refs_0_ = f32[1,256,512]{2,1,0:T(8,128)S(1)} collective-permute-done((f32[1,256,512]{2,1,0:T(8,128)S(1)}, f32[1,256,512]{2,1,0:T(8,128)S(1)}, u32[]{:S(2)}, u32[]{:S(2)}) %collective-permute-start.5) | collective-permute-done | bytes 524320 | tf_op jit(solution)/shard_map/ppermute | solution.py:554
  77.3 1.5 %collective-permute-start.7 = (f32[1,256,512]{2,1,0:T(8,128)S(1)}, f32[1,256,512]{2,1,0:T(8,128)S(1)}, u32[]{:S(2)}, u32[]{:S(2)}) collective-permute-start(f32[1,256,512]{2,1,0:T(8,128)S(1)} %slice_add_fusion.6), channel_id=1, source_target_pairs={{0,4},{1,3},{2,6},{3,1},{4,0},{5,7},{6,2},{7,5},{8,12},{9,11},{10,... | collective-permute-start | bytes 1572872 | tf_op jit(solution)/shard_map/ppermute | solution.py:542
  78.8 1.3 %collective-permute-start.9 = (f32[1,256,512]{2,1,0:T(8,128)S(1)}, f32[1,256,512]{2,1,0:T(8,128)S(1)}, u32[]{:S(2)}, u32[]{:S(2)}) collective-permute-start(f32[1,256,512]{2,1,0:T(8,128)S(1)} %collective-permute-done.6.refs_4_), channel_id=1, source_target_pairs={{8,0},{16,8},{24,16},{9,1},{17,9},{25,17},{10,2},{18,10},{26,18},{... | collective-permute-start | bytes 1572872 | tf_op jit(solution)/shard_map/ppermute | solution.py:558
  80.1 6.4 %collective-permute-done.7 = f32[1,256,512]{2,1,0:T(8,128)S(1)} collective-permute-done((f32[1,256,512]{2,1,0:T(8,128)S(1)}, f32[1,256,512]{2,1,0:T(8,128)S(1)}, u32[]{:S(2)}, u32[]{:S(2)}) %collective-permute-start.7) | collective-permute-done | bytes 524320 | tf_op jit(solution)/shard_map/ppermute | solution.py:542
  86.4 0.2 fusion.1.refs_3_.refs_2_
  86.7 5.2 %collective-permute-start.8 = (f32[1,256,512]{2,1,0:T(8,128)S(1)}, f32[1,256,512]{2,1,0:T(8,128)}, u32[]{:S(2)}, u32[]{:S(2)}) collective-permute-start(f32[1,256,512]{2,1,0:T(8,128)S(1)} %fusion.1.refs_3_.refs_2_), channel_id=1, source_target_pairs={{0,8},{8,16},{16,24},{1,9},{9,17},{17,25},{2,10},{10,18},{18,26},{... | collective-permute-start | bytes 1572872 | tf_op jit(solution)/shard_map/ppermute | solution.py:554
  91.8 1.3 %collective-permute-start.11 = (f32[1,256,512]{2,1,0:T(8,128)S(1)}, f32[1,256,512]{2,1,0:T(8,128)}, u32[]{:S(2)}, u32[]{:S(2)}) collective-permute-start(f32[1,256,512]{2,1,0:T(8,128)S(1)} %fusion.1.refs_3_.refs_2_), channel_id=1, source_target_pairs={{8,0},{16,8},{24,16},{9,1},{17,9},{25,17},{10,2},{18,10},{26,18},{... | collective-permute-start | bytes 1572872 | tf_op jit(solution)/shard_map/ppermute | solution.py:558
  93.1 5.5 %collective-permute-done.8.refs_1_ = f32[1,256,512]{2,1,0:T(8,128)} collective-permute-done((f32[1,256,512]{2,1,0:T(8,128)S(1)}, f32[1,256,512]{2,1,0:T(8,128)}, u32[]{:S(2)}, u32[]{:S(2)}) %collective-permute-start.8) | collective-permute-done | bytes 524320 | tf_op jit(solution)/shard_map/ppermute | solution.py:554
  98.6 4.5 %collective-permute-start.10 = (f32[1,256,512]{2,1,0:T(8,128)}, f32[1,256,512]{2,1,0:T(8,128)S(1)}, u32[]{:S(2)}, u32[]{:S(2)}) collective-permute-start(f32[1,256,512]{2,1,0:T(8,128)} %collective-permute-done.8.refs_1_), channel_id=1, source_target_pairs={{0,8},{8,16},{16,24},{1,9},{9,17},{17,25},{2,10},{10,18},{18,26},{... | collective-permute-start | bytes 1572872 | tf_op jit(solution)/shard_map/ppermute | solution.py:554
  103.2 0.1 copy.12.pairs
  103.3 0.4 collective-permute-done.11.refs_5_
  103.6 6.2 %cross.2 = (f32[2,4,2,128,512]{4,3,2,1,0:T(8,128)}, f32[2,4,2,128,512]{4,3,2,1,0:T(8,128)}) custom-call(s32[20,2]{1,0:T(8,128)S(1)} %copy.12.pairs, f32[1,256,512]{2,1,0:T(8,128)S(1)} %collective-permute-done.5.refs_0_, f32[1,256,512]{2,1,0:T(8,128)} %collective-permute-done.8.refs_1_, f32[1,256,512]{2,1,0:T(8,128)S(1)} %fusion.refs_2_.refs_1_, ...), custom_call_target="tpu_custom_call" | custom-call | flops 84148224 | bytes 10485760 | tf_op jit(solution)/shard_map/cross/pallas_call | solution.py:487
  109.8 0.3 collective-permute-done.10.refs_0_
  110.1 3.9 %cross.3 = (f32[2,4,2,128,512]{4,3,2,1,0:T(8,128)}, f32[2,4,2,128,512]{4,3,2,1,0:T(8,128)}) custom-call(s32[20,2]{1,0:T(8,128)S(1)} %copy.12.pairs, f32[1,256,512]{2,1,0:T(8,128)S(1)} %collective-permute-done.10.refs_0_, f32[1,256,512]{2,1,0:T(8,128)S(1)} %fusion.refs_2_.refs_1_, ...), custom_call_target="tpu_custom_call", output_to_operand_aliasing={{0}: (5, {}), {1}: (6, {})} | custom-call | flops 53215232 | bytes 3145728 | tf_op jit(solution)/shard_map/cross/pallas_call | solution.py:487
  (9 shorter events, 0.1 us)
Async XLA Ops:
  21.0 4.5 %collective-permute-start = (f32[4,256,512]{2,1,0:T(8,128)}, f32[4,256,512]{2,1,0:T(8,128)S(1)}, u32[]{:S(2)}, u32[]{:S(2)}) collective-permute-start(f32[4,256,512]{2,1,0:T(8,128)} %get-tuple-element.14), channel_id=1, source_target_pairs={{0,1},{1,0},{2,3},{3,2},{4,5},{5,4},{6,7},{7,6},{8,9},{9,8},{10,11... | collective-permute-start | bytes 6291464 | tf_op jit(solution)/shard_map/ppermute | solution.py:535
  26.9 23.5 %copy-start.1 = (f32[4,256,512]{2,1,0:T(8,128)S(1)}, f32[4,256,512]{2,1,0:T(8,128)}, u32[]{:S(2)}) copy-start(f32[4,256,512]{2,1,0:T(8,128)} %get-tuple-element.13) | copy-start | bytes 6291460
  26.9 23.4 %collective-permute-start.1 = (f32[2,256,512]{2,1,0:T(8,128)S(1)}, f32[2,256,512]{2,1,0:T(8,128)S(1)}, u32[]{:S(2)}, u32[]{:S(2)}) collective-permute-start(f32[2,256,512]{2,1,0:T(8,128)S(1)} %slice_add_fusion.1), channel_id=1, source_target_pairs={{0,2},{1,5},{2,0},{3,7},{4,6},{5,1},{6,4},{7,3},{8,10},{9,13},{10,... | collective-permute-start | bytes 3145736 | tf_op jit(solution)/shard_map/ppermute | solution.py:542
  50.3 4.5 %copy-start = (f32[4,256,512]{2,1,0:T(8,128)S(1)}, f32[4,256,512]{2,1,0:T(8,128)}, u32[]{:S(2)}) copy-start(f32[4,256,512]{2,1,0:T(8,128)} %get-tuple-element.11) | copy-start | bytes 6291460
  50.3 4.4 %collective-permute-start.2 = (f32[4,256,512]{2,1,0:T(8,128)}, f32[4,256,512]{2,1,0:T(8,128)S(1)}, u32[]{:S(2)}, u32[]{:S(2)}) collective-permute-start(f32[4,256,512]{2,1,0:T(8,128)} %get-tuple-element.15), channel_id=1, source_target_pairs={{0,1},{1,0},{2,3},{3,2},{4,5},{5,4},{6,7},{7,6},{8,9},{9,8},{10,11... | collective-permute-start | bytes 6291464 | tf_op jit(solution)/shard_map/ppermute | solution.py:535
  50.6 11.2 %collective-permute-start.4 = (f32[1,256,512]{2,1,0:T(8,128)S(1)}, f32[1,256,512]{2,1,0:T(8,128)S(1)}, u32[]{:S(2)}, u32[]{:S(2)}) collective-permute-start(f32[1,256,512]{2,1,0:T(8,128)S(1)} %slice_add_fusion.2), channel_id=1, source_target_pairs={{0,4},{1,3},{2,6},{3,1},{4,0},{5,7},{6,2},{7,5},{8,12},{9,11},{10,... | collective-permute-start | bytes 1572872 | tf_op jit(solution)/shard_map/ppermute | solution.py:542
  55.0 15.6 %collective-permute-start.3 = (f32[2,256,512]{2,1,0:T(8,128)S(1)}, f32[2,256,512]{2,1,0:T(8,128)S(1)}, u32[]{:S(2)}, u32[]{:S(2)}) collective-permute-start(f32[2,256,512]{2,1,0:T(8,128)S(1)} %slice_add_fusion), channel_id=1, source_target_pairs={{0,2},{1,5},{2,0},{3,7},{4,6},{5,1},{6,4},{7,3},{8,10},{9,13},{10,... | collective-permute-start | bytes 3145736 | tf_op jit(solution)/shard_map/ppermute | solution.py:542
  62.0 41.1 %copy-start.2 = (s32[20,2]{0,1:T(2,128)S(1)}, s32[20,2]{0,1:T(2,128)}, u32[]{:S(2)}) copy-start(s32[20,2]{0,1:T(2,128)} %param.9) | copy-start | bytes 484
  62.0 14.0 %collective-permute-start.6 = (f32[1,256,512]{2,1,0:T(8,128)S(1)}, f32[1,256,512]{2,1,0:T(8,128)S(1)}, u32[]{:S(2)}, u32[]{:S(2)}) collective-permute-start(f32[1,256,512]{2,1,0:T(8,128)S(1)} %fusion.refs_2_.refs_1_), channel_id=1, source_target_pairs={{8,0},{16,8},{24,16},{9,1},{17,9},{25,17},{10,2},{18,10},{26,18},{... | collective-permute-start | bytes 1572872 | tf_op jit(solution)/shard_map/ppermute | solution.py:558
  63.3 13.9 %collective-permute-start.5 = (f32[1,256,512]{2,1,0:T(8,128)S(1)}, f32[1,256,512]{2,1,0:T(8,128)S(1)}, u32[]{:S(2)}, u32[]{:S(2)}) collective-permute-start(f32[1,256,512]{2,1,0:T(8,128)S(1)} %fusion.refs_2_.refs_1_), channel_id=1, source_target_pairs={{0,8},{8,16},{16,24},{1,9},{9,17},{17,25},{2,10},{10,18},{18,26},{... | collective-permute-start | bytes 1572872 | tf_op jit(solution)/shard_map/ppermute | solution.py:554
  77.3 9.2 %collective-permute-start.7 = (f32[1,256,512]{2,1,0:T(8,128)S(1)}, f32[1,256,512]{2,1,0:T(8,128)S(1)}, u32[]{:S(2)}, u32[]{:S(2)}) collective-permute-start(f32[1,256,512]{2,1,0:T(8,128)S(1)} %slice_add_fusion.6), channel_id=1, source_target_pairs={{0,4},{1,3},{2,6},{3,1},{4,0},{5,7},{6,2},{7,5},{8,12},{9,11},{10,... | collective-permute-start | bytes 1572872 | tf_op jit(solution)/shard_map/ppermute | solution.py:542
  78.8 14.4 %collective-permute-start.9 = (f32[1,256,512]{2,1,0:T(8,128)S(1)}, f32[1,256,512]{2,1,0:T(8,128)S(1)}, u32[]{:S(2)}, u32[]{:S(2)}) collective-permute-start(f32[1,256,512]{2,1,0:T(8,128)S(1)} %collective-permute-done.6.refs_4_), channel_id=1, source_target_pairs={{8,0},{16,8},{24,16},{9,1},{17,9},{25,17},{10,2},{18,10},{26,18},{... | collective-permute-start | bytes 1572872 | tf_op jit(solution)/shard_map/ppermute | solution.py:558
  86.7 12.0 %collective-permute-start.8 = (f32[1,256,512]{2,1,0:T(8,128)S(1)}, f32[1,256,512]{2,1,0:T(8,128)}, u32[]{:S(2)}, u32[]{:S(2)}) collective-permute-start(f32[1,256,512]{2,1,0:T(8,128)S(1)} %fusion.1.refs_3_.refs_2_), channel_id=1, source_target_pairs={{0,8},{8,16},{16,24},{1,9},{9,17},{17,25},{2,10},{10,18},{18,26},{... | collective-permute-start | bytes 1572872 | tf_op jit(solution)/shard_map/ppermute | solution.py:554
  91.8 11.8 %collective-permute-start.11 = (f32[1,256,512]{2,1,0:T(8,128)S(1)}, f32[1,256,512]{2,1,0:T(8,128)}, u32[]{:S(2)}, u32[]{:S(2)}) collective-permute-start(f32[1,256,512]{2,1,0:T(8,128)S(1)} %fusion.1.refs_3_.refs_2_), channel_id=1, source_target_pairs={{8,0},{16,8},{24,16},{9,1},{17,9},{25,17},{10,2},{18,10},{26,18},{... | collective-permute-start | bytes 1572872 | tf_op jit(solution)/shard_map/ppermute | solution.py:558
  98.6 11.5 %collective-permute-start.10 = (f32[1,256,512]{2,1,0:T(8,128)}, f32[1,256,512]{2,1,0:T(8,128)S(1)}, u32[]{:S(2)}, u32[]{:S(2)}) collective-permute-start(f32[1,256,512]{2,1,0:T(8,128)} %collective-permute-done.8.refs_1_), channel_id=1, source_target_pairs={{0,8},{8,16},{16,24},{1,9},{9,17},{17,25},{2,10},{10,18},{18,26},{... | collective-permute-start | bytes 1572872 | tf_op jit(solution)/shard_map/ppermute | solution.py:554

commit v4 on v3

--- a/solution.py
+++ b/solution.py
@@ -15,7 +15,7 @@
 KZ = 1024
 LANES = 128
 GROUP = 8
-VMEM_LIMIT = 56 * 1024 * 1024
+MIB = 1024 * 1024
 F32 = jnp.float32
 BF16 = jnp.bfloat16
 
@@ -168,7 +168,7 @@
         copy.start()
 
 
-def span_phase(radix, plane, places, plane_slot, field, table, shift, y, scratch, after_pair):
+def span_phase(radix, plane, places, plane_slot, field, table, shift, y, scratch):
     velocity, span, turn, fold_high, fold_low, load_done, rest_done = scratch
     planes, rows, _ = field.shape
     shares = y.shape[0]
@@ -219,18 +219,16 @@
                 owned = slice(owner * 2 * GROUP, (owner + 1) * 2 * GROUP)
                 y[place, first : first + 2 * GROUP, :rows] = high[owned]
                 y[place, first : first + 2 * GROUP, rows:] = low[owned]
-        after_pair(number)
     yield
 
 
-def axial_phase(y, wave, total, sent, kept, out_done, before_group):
+def axial_phase(y, wave, total, sent, kept, out_done):
     shares, count, width = y.shape
     half_count = shares // 2
     rows = width // 2
     owners = shares // out_done.shape[0]
     leaving = []
     for first in range(0, shares, owners):
-        before_group(first // owners)
         left = y[first : first + owners].reshape(owners * count, width)
         value = dot_nn(left, wave[:width]) + dot_nn(left[:, :rows], wave[width:])
         window = pl.ds(first, owners)
@@ -243,42 +241,13 @@
 
 
 def whole_kernel(radix, plane, places, plane_slot, field, table, shift, axial, sent, kept, y, wave, total, wave_done, out_done, *scratch):
-    phase = span_phase(radix, plane, places, plane_slot, field, table, shift, y, scratch, lambda number: None)
+    phase = span_phase(radix, plane, places, plane_slot, field, table, shift, y, scratch)
     next(phase)
     load = pltpu.make_async_copy(axial.at[lax.axis_index("pencil")], wave, wave_done)
     load.start()
     next(phase)
     load.wait()
-    axial_phase(y, wave, total, sent, kept, out_done, lambda group: None)
-
-
-def span_kernel(radix, plane, places, plane_slot, field, table, shift, y_out, y, pair_done, *scratch):
-    height = y.shape[1] // (radix // 2)
-    copies = [
-        pltpu.make_async_copy(
-            y.at[:, pl.ds(number * height, height)], y_out.at[:, pl.ds(number * height, height)], pair_done.at[number]
-        )
-        for number in range(radix // 2)
-    ]
-    for _ in span_phase(
-        radix, plane, places, plane_slot, field, table, shift, y, scratch, lambda number: copies[number].start()
-    ):
-        pass
-    for copy in copies:
-        copy.wait()
-
-
-def axial_kernel(y_in, axial, sent, kept, y, wave, total, wave_done, out_done, in_done):
-    owners = y.shape[0] // out_done.shape[0]
-    load = pltpu.make_async_copy(axial.at[lax.axis_index("pencil")], wave, wave_done)
-    load.start()
-    copies = []
-    for group in range(out_done.shape[0]):
-        window = pl.ds(group * owners, owners)
-        copies.append(pltpu.make_async_copy(y_in.at[window], y.at[window], in_done.at[group]))
-    start_all(copies)
-    load.wait()
-    axial_phase(y, wave, total, sent, kept, out_done, lambda group: copies[group].wait())
+    axial_phase(y, wave, total, sent, kept, out_done)
 
 
 def transform_calls(planes, rows, nz, shares, radix):
@@ -294,7 +263,8 @@
     out = jax.ShapeDtypeStruct((half_count, count, KX), F32)
     modes = jax.ShapeDtypeStruct((shares, count, 2 * rows), BF16)
     smem = pl.BlockSpec(memory_space=pltpu.SMEM)
-    hbm = pl.BlockSpec(memory_space=pl.ANY)
+    hbm = pl.BlockSpec(memory_space=pltpu.HBM)
+    free = pl.BlockSpec(memory_space=pl.ANY)
     one, many = pltpu.SemaphoreType.DMA(()), lambda number: pltpu.SemaphoreType.DMA((number,))
     y = pltpu.VMEM(modes.shape, BF16)
     span_scratch = [
@@ -315,14 +285,14 @@
     span_cost = (3 * rows * pairs * table_rows * depth, rows * nz * 4 + pairs * table_rows * depth * 2)
     axial_cost = (6 * shares * count * rows * KX, shares * count * (KX + rows) * 4)
 
-    def call(kernel, name, costs, ins, outs, scratch):
+    def call(kernel, name, limit, costs, ins, outs, scratch):
         return pl.pallas_call(
             kernel,
             out_shape=outs,
             in_specs=ins,
-            out_specs=jax.tree.map(lambda _: hbm, outs),
+            out_specs=jax.tree.map(lambda _: free, outs),
             scratch_shapes=scratch,
-            compiler_params=pltpu.CompilerParams(vmem_limit_bytes=VMEM_LIMIT),
+            compiler_params=pltpu.CompilerParams(vmem_limit_bytes=limit),
             cost_estimate=pl.CostEstimate(
                 flops=sum(cost[0] for cost in costs), bytes_accessed=sum(cost[1] for cost in costs), transcendentals=0
             ),
@@ -333,40 +303,61 @@
         return call(
             functools.partial(whole_kernel, radix, plane),
             "whole",
+            40 * MIB if plane else 56 * MIB,
             [span_cost, axial_cost],
-            [smem, smem, hbm, hbm, hbm, hbm],
+            [smem, smem, hbm, free if plane else hbm, hbm, hbm],
             (out, out),
             [y] + axial_scratch + span_scratch,
         )(places, plane_slot, field, table, shift, axial)
 
-    def span(plane, plane_slot, field):
-        return call(
-            functools.partial(span_kernel, radix, plane),
-            "span",
-            [span_cost],
-            [smem, smem, hbm, hbm, hbm],
-            modes,
-            [y, many(pairs)] + span_scratch,
-        )(places, plane_slot, field, table, shift)
-
-    def along_x(spanned):
-        return call(
-            axial_kernel,
-            "axial",
-            [axial_cost],
-            [hbm, hbm],
-            (out, out),
-            [y] + axial_scratch + [many(shares // owners)],
-        )(spanned, axial)
-
-    return whole, span, along_x
-
-
-def cross_kernel(radix, planes, offsets, band_slots, partner_slots, pairs, *refs):
+    return whole
+
+
+def residues(radix):
+    return [residue for pair in class_pairs(radix) for residue in pair]
+
+
+def mirror_matrix():
+    row = lax.broadcasted_iota(jnp.int32, (LANES, LANES), 0)
+    column = lax.broadcasted_iota(jnp.int32, (LANES, LANES), 1)
+    return (row + column == LANES - 1).astype(BF16)
+
+
+def spectrum(radix, value, side, store):
+    share = radix * GROUP
+    value = value.reshape(radix // 2, 2, 2 * GROUP, 2 * LANES)
+    re_rows = value[:, 0].reshape(share, 2 * LANES)
+    im_rows = value[:, 1].reshape(share, 2 * LANES)
+    re_cos, re_sin = re_rows[:, :LANES], re_rows[:, LANES:]
+    im_cos, im_sin = im_rows[:, :LANES], im_rows[:, LANES:]
+    if side == 0:
+        parts = (re_cos + im_sin, im_cos - re_sin)
+    else:
+        mirror = mirror_matrix()
+
+        def mirrored(part):
+            high = part.astype(BF16)
+            middle, low = split(part - high.astype(F32))
+            return dot_nn(high, mirror) + dot_nn(middle, mirror) + dot_nn(low, mirror)
+
+        parts = (mirrored(re_cos - im_sin), mirrored(im_cos + re_sin))
+    for part in range(2):
+        for number, residue in enumerate(residues(radix)):
+            store(part, pl.ds(residue, GROUP, stride=radix), parts[part][number * GROUP : (number + 1) * GROUP])
+
+
+def products(end, own, far):
+    own_re, own_im = own
+    far_re, far_im = far
+    if end == 0:
+        return own_re * far_re + own_im * far_im, own_im * far_re - own_re * far_im
+    return far_re * own_re + far_im * own_im, far_re * own_im - far_im * own_re
+
+
+def cross_kernel(radix, planes, offsets, slots, pairs, *refs):
     sources = dict(zip(offsets, refs[: len(offsets)]))
-    band_out, partner_out, wanted, woven = refs[-4:]
+    outs, wanted, woven = refs[-4:-2], refs[-2], refs[-1]
     band = wanted.shape[0] // (2 * planes)
-    share = woven.shape[2]
     side = pl.program_id(1)
 
     @pl.when((pl.program_id(0) == 0) & (side == 0))
@@ -392,117 +383,104 @@
 
         lax.fori_loop(0, pairs.shape[0], mark, 0)
 
-    residues = [residue for pair in class_pairs(radix) for residue in pair]
-
-    def parts(source):
-        value = source[0].reshape(radix // 2, 2, 2 * GROUP, 2 * LANES)
-        re_rows = value[:, 0].reshape(share, 2 * LANES)
-        im_rows = value[:, 1].reshape(share, 2 * LANES)
-        return re_rows[:, :LANES], re_rows[:, LANES:], im_rows[:, :LANES], im_rows[:, LANES:]
-
-    def weave(index, values):
-        for part in range(2):
-            for number, residue in enumerate(residues):
-                woven[index, part, pl.ds(residue, GROUP, stride=radix), :] = values[part][
-                    number * GROUP : (number + 1) * GROUP
-                ]
-
-    @pl.when(side == 0)
-    def _():
-        for index, offset in enumerate(offsets):
-            re_cos, re_sin, im_cos, im_sin = parts(sources[offset])
-            weave(index, (re_cos + im_sin, im_cos - re_sin))
-
-    @pl.when(side == 1)
-    def _():
-        row = lax.broadcasted_iota(jnp.int32, (LANES, LANES), 0)
-        column = lax.broadcasted_iota(jnp.int32, (LANES, LANES), 1)
-        mirror = (row + column == LANES - 1).astype(BF16)
-
-        def mirrored(value):
-            high = value.astype(BF16)
-            middle, low = split(value - high.astype(F32))
-            return dot_nn(high, mirror) + dot_nn(middle, mirror) + dot_nn(low, mirror)
-
-        for index, offset in enumerate(offsets):
-            re_cos, re_sin, im_cos, im_sin = parts(sources[offset])
-            weave(index, (mirrored(re_cos - im_sin), mirrored(im_cos + re_sin)))
-
-    def spectrum(offset):
+    def weave(index, part, rows, value):
+        woven[index, part, rows, :] = value
+
+    for value in range(2):
+
+        @pl.when(side == value)
+        def _():
+            for index, offset in enumerate(offsets):
+                spectrum(radix, sources[offset][0], value, functools.partial(weave, index))
+
+    def woven_parts(offset):
         index = offsets.index(offset)
         return woven[index, 0], woven[index, 1]
 
-    for out, slots, end in ((band_out, band_slots, 0), (partner_out, partner_slots, 1)):
-        for place, own, gap in slots:
-            keep = wanted[(end * planes + own) * band + gap] != 0
-            own_re, own_im = spectrum(own)
-            if end == 0:
-                far_re, far_im = spectrum(own + gap)
-                imag = own_im * far_re - own_re * far_im
-            else:
-                far_re, far_im = spectrum(own - gap)
-                imag = far_re * own_im - far_im * own_re
-            out[place + (0,)] = jnp.where(keep, own_re * far_re + own_im * far_im, 0.0)
-            out[place + (1,)] = jnp.where(keep, imag, 0.0)
-
-
-def cross(pairs, sources, earlier, planes, band, radix, last):
+    for end, own, gap in slots:
+        keep = wanted[(end * planes + own) * band + gap] != 0
+        far = own + gap if end == 0 else own - gap
+        for part, value in enumerate(products(end, woven_parts(own), woven_parts(far))):
+            outs[end][own, gap, part] = jnp.where(keep, value, 0.0)
+
+
+def cross(pairs, near, planes, band, radix):
     share = radix * GROUP
     blocks = KX // 2 // LANES
+    slots = [
+        (end, own, gap)
+        for own in range(planes)
+        for gap in range(band)
+        for end in range(2)
+        if (own + gap if end == 0 else own - gap) in near
+    ]
+    offsets = sorted(near)
     out = jax.ShapeDtypeStruct((planes, band, 2, share, KX), F32)
-
-    def lane_block(block, side):
-        return block + side * (2 * blocks - 1 - 2 * block)
-
-    slots = {0: [], 1: []}
-    if last:
-        places = {0: (planes - 1, band - 1), 1: (0, band - 1)}
-        slots = {0: [((0, 0), planes - 1, band - 1)], 1: [((0, 0), 0, band - 1)]}
-        out_specs = tuple(
-            pl.BlockSpec(
-                (1, 1, 2, share, LANES),
-                functools.partial(lambda end, b, side: places[end] + (0, 0, lane_block(b, side)), end),
-            )
-            for end in range(2)
-        )
-    else:
-        for own in range(planes):
-            for gap in range(band):
-                for end in range(2):
-                    far = own + gap if end == 0 else own - gap
-                    if far in sources:
-                        slots[end].append(((own, gap), own, gap))
-        spec = pl.BlockSpec(
-            (planes, band, 2, share, LANES), lambda b, side: (0, 0, 0, 0, lane_block(b, side))
-        )
-        out_specs = (spec, spec)
-    used = sorted(
-        {own for end in range(2) for _, own, _ in slots[end]}
-        | {own + gap for _, own, gap in slots[0]}
-        | {own - gap for _, own, gap in slots[1]}
+    spec = pl.BlockSpec(
+        (planes, band, 2, share, LANES), lambda b, side: (0, 0, 0, 0, b + side * (2 * blocks - 1 - 2 * b))
     )
-    specs = [pl.BlockSpec(memory_space=pltpu.SMEM)]
-    specs += [pl.BlockSpec((1, 2 * share, 2 * LANES), lambda b, side: (0, 0, b))] * len(used)
-    specs += [pl.BlockSpec(memory_space=pl.ANY)] * len(earlier)
+    smem = pl.BlockSpec(memory_space=pltpu.SMEM)
     return pl.pallas_call(
-        functools.partial(cross_kernel, radix, planes, used, slots[0], slots[1]),
-        out_shape=(out, out),
+        functools.partial(cross_kernel, radix, planes, offsets, slots),
+        out_shape=(out, out, jax.ShapeDtypeStruct((2 * planes * band,), jnp.int32)),
         grid=(blocks, 2),
-        in_specs=specs,
-        out_specs=out_specs,
-        scratch_shapes=[
-            pltpu.SMEM((2 * planes * band,), jnp.int32),
-            pltpu.VMEM((len(used), 2, share, LANES), F32),
-        ],
-        input_output_aliases={1 + len(used) + i: i for i in range(len(earlier))},
-        compiler_params=pltpu.CompilerParams(vmem_limit_bytes=48 * 1024 * 1024),
+        in_specs=[smem] + [pl.BlockSpec((1, 2 * share, 2 * LANES), lambda b, side: (0, 0, b))] * len(offsets),
+        out_specs=(spec, spec, smem),
+        scratch_shapes=[pltpu.VMEM((len(offsets), 2, share, LANES), F32)],
+        compiler_params=pltpu.CompilerParams(vmem_limit_bytes=32 * MIB),
         cost_estimate=pl.CostEstimate(
-            flops=(len(slots[0]) + len(slots[1])) * share * KX * 6 + len(used) * share * KX * 200,
-            bytes_accessed=(len(slots[0]) + len(slots[1]) + len(used)) * share * KX * 8,
+            flops=len(slots) * share * KX * 6 + len(offsets) * share * KX * 200,
+            bytes_accessed=(len(slots) + len(offsets)) * share * KX * 8,
             transcendentals=0,
         ),
         name="cross",
-    )(pairs, *[sources[offset] for offset in used], *earlier)
+    )(pairs, *[near[offset] for offset in offsets])
+
+
+def cross_last_kernel(radix, planes, band, wanted, *refs):
+    sources, outs, woven = refs[:4], refs[-3:-1], refs[-1]
+    blocks = KX // 2 // LANES
+    for end in range(2):
+        own = planes - 1 if end == 0 else 0
+        keep = wanted[(end * planes + own) * band + band - 1] != 0
+        for block in range(blocks):
+            for side in range(2):
+                place = block if side == 0 else 2 * blocks - 1 - block
+                lanes = slice(place * LANES, (place + 1) * LANES)
+                columns = slice(block * 2 * LANES, (block + 1) * 2 * LANES)
+                for index in range(2):
+
+                    def weave(part, rows, value):
+                        woven[end, place, index, part, rows, :] = value
+
+                    spectrum(radix, sources[2 * end + index][0, :, columns], side, weave)
+                spectra = [(woven[end, place, index, 0], woven[end, place, index, 1]) for index in range(2)]
+                for part, value in enumerate(products(end, *spectra)):
+                    outs[end][0, 0, part, :, lanes] = jnp.where(keep, value, 0.0)
+
+
+def cross_last(wanted, sources, earlier, planes, band, radix):
+    share = radix * GROUP
+    out = jax.ShapeDtypeStruct((planes, band, 2, share, KX), F32)
+    whole = pl.BlockSpec((1, 2 * share, KX), lambda i: (0, 0, 0))
+    places = ((planes - 1, band - 1), (0, band - 1))
+    return pl.pallas_call(
+        functools.partial(cross_last_kernel, radix, planes, band),
+        out_shape=(out, out),
+        grid=(1,),
+        in_specs=[pl.BlockSpec(memory_space=pltpu.SMEM)] + [whole] * 4 + [pl.BlockSpec(memory_space=pl.ANY)] * 2,
+        out_specs=tuple(
+            pl.BlockSpec((1, 1, 2, share, KX), functools.partial(lambda place, i: place + (0, 0, 0), place))
+            for place in places
+        ),
+        scratch_shapes=[pltpu.VMEM((2, KX // LANES, 2, 2, share, LANES), F32)],
+        input_output_aliases={5: 0, 6: 1},
+        compiler_params=pltpu.CompilerParams(vmem_limit_bytes=32 * MIB),
+        cost_estimate=pl.CostEstimate(
+            flops=share * KX * 900, bytes_accessed=8 * share * KX * 8, transcendentals=0
+        ),
+        name="cross_last",
+    )(wanted, *sources, *earlier)
 
 
 def solution(mesh):
@@ -521,7 +499,7 @@
     def local(velocity, plane_slot, pair_list):
         planes, rows, nz = velocity.shape
         band = planes * reach
-        whole, span, along_x = transform_calls(planes, rows, nz, shares, radix)
+        whole = transform_calls(planes, rows, nz, shares, radix)
 
         def after(value, *earlier):
             return lax.optimization_barrier((value,) + earlier)[0]
@@ -559,8 +537,9 @@
                     home[plane + away * planes] = above
                     first_hops.append(above)
             first_hops = first_hops[:2]
-        outputs = cross(pair_list, near, (), planes, band, radix, False)
-        return tuple(cross(pair_list, {**near, **far}, outputs, planes, band, radix, True))
+        *outputs, wanted = cross(pair_list, near, planes, band, radix)
+        sources = [near[planes - 1], far[planes - 1 + band - 1], near[0], far[1 - band]]
+        return tuple(cross_last(wanted, sources, outputs, planes, band, radix))
 
     return jax.shard_map(
         local,

time: 114 us -> 112 us (0.982)
  Pallas kernels: 50.8 us -> 48.5 us
    pallas_call x4, Pallas kernels: 50.8 us -> 48.5 us  [the longest x2 39.2 us: whole(): call(functools.partial(whole_kernel, radix, plane), 'whole', 40 * MIB if...]
  transfers between devices with their start and end apart: 12 -> 12, of which waited for: 10 -> 8; matrix products, arithmetic and copies ran while one was open for 1% -> 1% of each run, Pallas kernels for 23% -> 22%
where the time goes in v4:
time: 112 us
  Pallas kernels  48.5 us (43%)
  waiting for transfers between devices  33.7 us (30%)
  starting transfers between devices  25.7 us (23%)
  other arithmetic  2.36 us (2%)
    pallas_call x2, Pallas kernels, whole(): call(functools.partial(whole_kernel, radix, plane), 'whole', 40 * MIB if...  39.2 us
    ppermute x4, waiting for transfers between devices, local(): terms.append(lax.ppermute(leaving, 'pencil', swap))  15 us
    ppermute x3, starting transfers between devices, local(): below = lax.ppermute(below, 'plane', upward)  14.2 us
    ppermute x4, starting transfers between devices, local(): terms.append(lax.ppermute(leaving, 'pencil', swap))  7.09 us
    ppermute x3, waiting for transfers between devices, local(): below = lax.ppermute(below, 'plane', upward)  6.74 us
    ppermute x2, waiting for transfers between devices, local(): terms = [kept, lax.ppermute(sent, 'pencil', core_swap)]  6.4 us
    pallas_call x1, Pallas kernels, cross(): pl.pallas_call(functools.partial(cross_kernel, radix, planes, offsets, sl...  6.18 us
    ppermute x3, waiting for transfers between devices, local(): above = lax.ppermute(above, 'plane', downward)  5.56 us
  transfers between devices with their start and end apart: 12, of which 8 were waited for; matrix products, arithmetic and copies ran while one was open for 1% of the time, Pallas kernels for 22%

profile of v4, /device:TPU:0, one launch (start us, length us, event | category | flops | bytes accessed | tf_op | source)
XLA Modules:
  0.0 112.0 jit_solution(1132461284531335104)
XLA Ops:
  0.6 20.8 %whole.2 = (f32[4,256,512]{2,1,0:T(8,128)}, f32[4,256,512]{2,1,0:T(8,128)}) custom-call(s32[64]{0:T(128)} %constant.8.clone.places, s32[8]{0:T(128)} %plane_slot.3, f32[2,640,3840]{2,1,0:T(8,128)} %field.3, bf16[8,512,512]{2,1,0:T(8,128)(2,1)} %constant.9.clone.table, f32[8,8,640]{2,1,0:T(8,128)} %constant.10.clone.shift, ...), custom_call_target="tpu_custom_call" | custom-call | flops 8053063680 | bytes 23461888 | tf_op jit(solution)/shard_map/whole/pallas_call | solution.py:303
  21.5 0.5 collective-permute-start
  22.0 4.0 %collective-permute-done = f32[4,256,512]{2,1,0:T(8,128)S(1)} collective-permute-done((f32[4,256,512]{2,1,0:T(8,128)}, f32[4,256,512]{2,1,0:T(8,128)S(1)}, u32[]{:S(2)}, u32[]{:S(2)}) %collective-permute-start) | collective-permute-done | bytes 2097184 | tf_op jit(solution)/shard_map/ppermute | solution.py:513
  26.0 1.4 %slice_add_fusion.1 = f32[2,256,512]{2,1,0:T(8,128)S(1)} fusion(f32[4,256,512]{2,1,0:T(8,128)S(1)} %collective-permute-done, f32[4,256,512]{2,1,0:T(8,128)} %get-tuple-element.12), kind=kLoop, calls=%fused_computation.1 | loop fusion | flops 262144 | bytes 3145728 | tf_op jit(solution)/shard_map/add | solution.py:517
  27.5 2.9 %collective-permute-start.1 = (f32[2,256,512]{2,1,0:T(8,128)S(1)}, f32[2,256,512]{2,1,0:T(8,128)S(1)}, u32[]{:S(2)}, u32[]{:S(2)}) collective-permute-start(f32[2,256,512]{2,1,0:T(8,128)S(1)} %slice_add_fusion.1), channel_id=1, source_target_pairs={{0,2},{1,5},{2,0},{3,7},{4,6},{5,1},{6,4},{7,3},{8,10},{9,13},{10,... | collective-permute-start | bytes 3145736 | tf_op jit(solution)/shard_map/ppermute | solution.py:520
  30.4 18.4 %whole.3 = (f32[4,256,512]{2,1,0:T(8,128)S(1)}, f32[4,256,512]{2,1,0:T(8,128)S(1)}) custom-call(s32[64]{0:T(128)S(1)} %copy-done.5, s32[8]{0:T(128)S(1)} %copy-done.4, f32[2,640,3840]{2,1,0:T(8,128)} %field.3, bf16[8,512,512]{2,1,0:T(8,128)(2,1)S(1)} %copy-done, f32[8,8,640]{2,1,0:T(8,128)S(1)} %copy-done.1, bf16[8,1920,512]{2,1,0:T(8,128)(2,1)} %constant.11.clone.axial), custom_call_target="tpu_custom_call" | custom-call | flops 8053063680 | bytes 23461888 | tf_op jit(solution)/shard_map/whole/pallas_call | solution.py:303
  48.8 0.1 collective-permute-start.4
  48.9 0.1 slice_add_fusion.6
  49.0 1.6 %collective-permute-start.2 = (f32[1,256,512]{2,1,0:T(8,128)S(1)}, f32[1,256,512]{2,1,0:T(8,128)S(1)}, u32[]{:S(2)}, u32[]{:S(2)}) collective-permute-start(f32[1,256,512]{2,1,0:T(8,128)S(1)} %slice_add_fusion.6), channel_id=1, source_target_pairs={{0,4},{1,3},{2,6},{3,1},{4,0},{5,7},{6,2},{7,5},{8,12},{9,11},{10,... | collective-permute-start | bytes 1572872 | tf_op jit(solution)/shard_map/ppermute | solution.py:520
  50.6 2.4 %collective-permute-done.4 = f32[4,256,512]{2,1,0:T(8,128)S(1)} collective-permute-done((f32[4,256,512]{2,1,0:T(8,128)S(1)}, f32[4,256,512]{2,1,0:T(8,128)S(1)}, u32[]{:S(2)}, u32[]{:S(2)}) %collective-permute-start.4) | collective-permute-done | bytes 2097184 | tf_op jit(solution)/shard_map/ppermute | solution.py:513
  53.0 0.2 slice_add_fusion
  53.2 1.1 collective-permute-start.5
  54.3 6.2 %collective-permute-done.2 = f32[1,256,512]{2,1,0:T(8,128)S(1)} collective-permute-done((f32[1,256,512]{2,1,0:T(8,128)S(1)}, f32[1,256,512]{2,1,0:T(8,128)S(1)}, u32[]{:S(2)}, u32[]{:S(2)}) %collective-permute-start.2) | collective-permute-done | bytes 524320 | tf_op jit(solution)/shard_map/ppermute | solution.py:520
  60.5 0.2 fusion.1.refs_2_
  60.7 1.3 %collective-permute-start.6 = (f32[1,256,512]{2,1,0:T(8,128)S(1)}, f32[1,256,512]{2,1,0:T(8,128)S(1)}, u32[]{:S(2)}, u32[]{:S(2)}) collective-permute-start(f32[1,256,512]{2,1,0:T(8,128)S(1)} %fusion.1.refs_2_), channel_id=1, source_target_pairs={{8,0},{16,8},{24,16},{9,1},{17,9},{25,17},{10,2},{18,10},{26,18},{... | collective-permute-start | bytes 1572872 | tf_op jit(solution)/shard_map/ppermute | solution.py:536
  62.0 4.6 %collective-permute-start.3 = (f32[1,256,512]{2,1,0:T(8,128)S(1)}, f32[1,256,512]{2,1,0:T(8,128)S(1)}, u32[]{:S(2)}, u32[]{:S(2)}) collective-permute-start(f32[1,256,512]{2,1,0:T(8,128)S(1)} %fusion.1.refs_2_), channel_id=1, source_target_pairs={{0,8},{8,16},{16,24},{1,9},{9,17},{17,25},{2,10},{10,18},{18,26},{... | collective-permute-start | bytes 1572872 | tf_op jit(solution)/shard_map/ppermute | solution.py:532
  66.6 2.4 %collective-permute-done.5 = f32[2,256,512]{2,1,0:T(8,128)S(1)} collective-permute-done((f32[2,256,512]{2,1,0:T(8,128)S(1)}, f32[2,256,512]{2,1,0:T(8,128)S(1)}, u32[]{:S(2)}, u32[]{:S(2)}) %collective-permute-start.5) | collective-permute-done | bytes 1048608 | tf_op jit(solution)/shard_map/ppermute | solution.py:520
  69.0 0.1 slice_add_fusion.2
  69.2 5.6 %collective-permute-done.6.refs_4_ = f32[1,256,512]{2,1,0:T(8,128)S(1)} collective-permute-done((f32[1,256,512]{2,1,0:T(8,128)S(1)}, f32[1,256,512]{2,1,0:T(8,128)S(1)}, u32[]{:S(2)}, u32[]{:S(2)}) %collective-permute-start.6) | collective-permute-done | bytes 524320 | tf_op jit(solution)/shard_map/ppermute | solution.py:536
  74.7 1.2 %collective-permute-done.3.refs_0_ = f32[1,256,512]{2,1,0:T(8,128)S(1)} collective-permute-done((f32[1,256,512]{2,1,0:T(8,128)S(1)}, f32[1,256,512]{2,1,0:T(8,128)S(1)}, u32[]{:S(2)}, u32[]{:S(2)}) %collective-permute-start.3) | collective-permute-done | bytes 524320 | tf_op jit(solution)/shard_map/ppermute | solution.py:532
  75.9 1.5 %collective-permute-start.7 = (f32[1,256,512]{2,1,0:T(8,128)S(1)}, f32[1,256,512]{2,1,0:T(8,128)S(1)}, u32[]{:S(2)}, u32[]{:S(2)}) collective-permute-start(f32[1,256,512]{2,1,0:T(8,128)S(1)} %slice_add_fusion.2), channel_id=1, source_target_pairs={{0,4},{1,3},{2,6},{3,1},{4,0},{5,7},{6,2},{7,5},{8,12},{9,11},{10,... | collective-permute-start | bytes 1572872 | tf_op jit(solution)/shard_map/ppermute | solution.py:520
  77.4 1.3 %collective-permute-start.10 = (f32[1,256,512]{2,1,0:T(8,128)S(1)}, f32[1,256,512]{2,1,0:T(8,128)S(1)}, u32[]{:S(2)}, u32[]{:S(2)}) collective-permute-start(f32[1,256,512]{2,1,0:T(8,128)S(1)} %collective-permute-done.6.refs_4_), channel_id=1, source_target_pairs={{8,0},{16,8},{24,16},{9,1},{17,9},{25,17},{10,2},{18,10},{26,18},{... | collective-permute-start | bytes 1572872 | tf_op jit(solution)/shard_map/ppermute | solution.py:536
  78.7 6.4 %collective-permute-done.7 = f32[1,256,512]{2,1,0:T(8,128)S(1)} collective-permute-done((f32[1,256,512]{2,1,0:T(8,128)S(1)}, f32[1,256,512]{2,1,0:T(8,128)S(1)}, u32[]{:S(2)}, u32[]{:S(2)}) %collective-permute-start.7) | collective-permute-done | bytes 524320 | tf_op jit(solution)/shard_map/ppermute | solution.py:520
  85.1 0.2 fusion.refs_3_.refs_0_
  85.3 4.4 %collective-permute-start.8 = (f32[1,256,512]{2,1,0:T(8,128)S(1)}, f32[1,256,512]{2,1,0:T(8,128)S(1)}, u32[]{:S(2)}, u32[]{:S(2)}) collective-permute-start(f32[1,256,512]{2,1,0:T(8,128)S(1)} %fusion.refs_3_.refs_0_), channel_id=1, source_target_pairs={{0,8},{8,16},{16,24},{1,9},{9,17},{17,25},{2,10},{10,18},{18,26},{... | collective-permute-start | bytes 1572872 | tf_op jit(solution)/shard_map/ppermute | solution.py:532
  89.7 1.3 %collective-permute-start.9 = (f32[1,256,512]{2,1,0:T(8,128)S(1)}, f32[1,256,512]{2,1,0:T(8,128)S(1)}, u32[]{:S(2)}, u32[]{:S(2)}) collective-permute-start(f32[1,256,512]{2,1,0:T(8,128)S(1)} %fusion.refs_3_.refs_0_), channel_id=1, source_target_pairs={{8,0},{16,8},{24,16},{9,1},{17,9},{25,17},{10,2},{18,10},{26,18},{... | collective-permute-start | bytes 1572872 | tf_op jit(solution)/shard_map/ppermute | solution.py:536
  91.1 0.8 copy-done.2
  91.9 5.6 %collective-permute-done.8.refs_1_ = f32[1,256,512]{2,1,0:T(8,128)S(1)} collective-permute-done((f32[1,256,512]{2,1,0:T(8,128)S(1)}, f32[1,256,512]{2,1,0:T(8,128)S(1)}, u32[]{:S(2)}, u32[]{:S(2)}) %collective-permute-start.8) | collective-permute-done | bytes 524320 | tf_op jit(solution)/shard_map/ppermute | solution.py:532
  97.4 5.2 %collective-permute-start.11 = (f32[1,256,512]{2,1,0:T(8,128)S(1)}, f32[1,256,512]{2,1,0:T(8,128)}, u32[]{:S(2)}, u32[]{:S(2)}) collective-permute-start(f32[1,256,512]{2,1,0:T(8,128)S(1)} %collective-permute-done.8.refs_1_), channel_id=1, source_target_pairs={{0,8},{8,16},{16,24},{1,9},{9,17},{17,25},{2,10},{10,18},{18,26},{... | collective-permute-start | bytes 1572872 | tf_op jit(solution)/shard_map/ppermute | solution.py:532
  102.6 0.1 copy.11.pairs
  102.7 6.2 %cross.1 = (f32[2,4,2,128,512]{4,3,2,1,0:T(8,128)}, f32[2,4,2,128,512]{4,3,2,1,0:T(8,128)}, s32[16]{0:T(128)S(1)}) custom-call(s32[20,2]{1,0:T(8,128)S(1)} %copy.11.pairs, f32[1,256,512]{2,1,0:T(8,128)S(1)} %collective-permute-done.3.refs_0_, f32[1,256,512]{2,1,0:T(8,128)S(1)} %collective-permute-done.8.refs_1_, f32[1,256,512]{2,1,0:T(8,128)S(1)} %fusion.1.refs_2_, ...), custom_call_target="tpu_custom_call" | custom-call | flops 84148224 | bytes 10485760 | tf_op jit(solution)/shard_map/cross/pallas_call | solution.py:423
  108.9 3.2 %cross_last.1 = (f32[2,4,2,128,512]{4,3,2,1,0:T(8,128)}, f32[2,4,2,128,512]{4,3,2,1,0:T(8,128)}) custom-call(s32[16]{0:T(128)S(1)} %get-tuple-element.18.wanted, f32[1,256,512]{2,1,0:T(8,128)S(1)} %fusion.refs_3_.refs_0_, f32[1,256,512]{2,1,0:T(8,128)S(1)} %copy-done.3, ...), custom_call_target="tpu_custom_call", output_to_operand_aliasing={{0}: (5, {}), {1}: (6, {})} | custom-call | flops 58982400 | bytes 4194304 | tf_op jit(solution)/shard_map/cross_last/pallas_call | solution.py:467
  (19 shorter events, 0.1 us)
Async XLA Ops:
  0.6 29.8 %copy-start = (bf16[8,512,512]{2,1,0:T(8,128)(2,1)S(1)}, bf16[8,512,512]{2,1,0:T(8,128)(2,1)}, u32[]{:S(2)}) copy-start(bf16[8,512,512]{2,1,0:T(8,128)(2,1)} %constant.9.clone.table) | copy-start | bytes 12582916
  21.5 8.9 %copy-start.1 = (f32[8,8,640]{2,1,0:T(8,128)S(1)}, f32[8,8,640]{2,1,0:T(8,128)}, u32[]{:S(2)}) copy-start(f32[8,8,640]{2,1,0:T(8,128)} %constant.10.clone.shift) | copy-start | bytes 491524
  21.5 8.9 %copy-start.4 = (s32[8]{0:T(128)S(1)}, s32[8]{0:T(128)}, u32[]{:S(2)}) copy-start(s32[8]{0:T(128)} %plane_slot.3) | copy-start | bytes 100
  21.5 8.9 %copy-start.5 = (s32[64]{0:T(128)S(1)}, s32[64]{0:T(128)}, u32[]{:S(2)}) copy-start(s32[64]{0:T(128)} %constant.8.clone.places) | copy-start | bytes 772
  21.5 4.5 %collective-permute-start = (f32[4,256,512]{2,1,0:T(8,128)}, f32[4,256,512]{2,1,0:T(8,128)S(1)}, u32[]{:S(2)}, u32[]{:S(2)}) collective-permute-start(f32[4,256,512]{2,1,0:T(8,128)} %get-tuple-element.13), channel_id=1, source_target_pairs={{0,1},{1,0},{2,3},{3,2},{4,5},{5,4},{6,7},{7,6},{8,9},{9,8},{10,11... | collective-permute-start | bytes 6291464 | tf_op jit(solution)/shard_map/ppermute | solution.py:513
  27.4 21.4 %copy-start.6 = (f32[4,256,512]{2,1,0:T(8,128)S(1)}, f32[4,256,512]{2,1,0:T(8,128)}, u32[]{:S(2)}) copy-start(f32[4,256,512]{2,1,0:T(8,128)} %get-tuple-element.12) | copy-start | bytes 6291460
  27.5 21.3 %collective-permute-start.1 = (f32[2,256,512]{2,1,0:T(8,128)S(1)}, f32[2,256,512]{2,1,0:T(8,128)S(1)}, u32[]{:S(2)}, u32[]{:S(2)}) collective-permute-start(f32[2,256,512]{2,1,0:T(8,128)S(1)} %slice_add_fusion.1), channel_id=1, source_target_pairs={{0,2},{1,5},{2,0},{3,7},{4,6},{5,1},{6,4},{7,3},{8,10},{9,13},{10,... | collective-permute-start | bytes 3145736 | tf_op jit(solution)/shard_map/ppermute | solution.py:520
  48.8 4.2 %collective-permute-start.4 = (f32[4,256,512]{2,1,0:T(8,128)S(1)}, f32[4,256,512]{2,1,0:T(8,128)S(1)}, u32[]{:S(2)}, u32[]{:S(2)}) collective-permute-start(f32[4,256,512]{2,1,0:T(8,128)S(1)} %get-tuple-element.16), channel_id=1, source_target_pairs={{0,1},{1,0},{2,3},{3,2},{4,5},{5,4},{6,7},{7,6},{8,9},{9,8},{10,11... | collective-permute-start | bytes 6291464 | tf_op jit(solution)/shard_map/ppermute | solution.py:513
  49.0 11.4 %collective-permute-start.2 = (f32[1,256,512]{2,1,0:T(8,128)S(1)}, f32[1,256,512]{2,1,0:T(8,128)S(1)}, u32[]{:S(2)}, u32[]{:S(2)}) collective-permute-start(f32[1,256,512]{2,1,0:T(8,128)S(1)} %slice_add_fusion.6), channel_id=1, source_target_pairs={{0,4},{1,3},{2,6},{3,1},{4,0},{5,7},{6,2},{7,5},{8,12},{9,11},{10,... | collective-permute-start | bytes 1572872 | tf_op jit(solution)/shard_map/ppermute | solution.py:520
  53.2 15.8 %collective-permute-start.5 = (f32[2,256,512]{2,1,0:T(8,128)S(1)}, f32[2,256,512]{2,1,0:T(8,128)S(1)}, u32[]{:S(2)}, u32[]{:S(2)}) collective-permute-start(f32[2,256,512]{2,1,0:T(8,128)S(1)} %slice_add_fusion), channel_id=1, source_target_pairs={{0,2},{1,5},{2,0},{3,7},{4,6},{5,1},{6,4},{7,3},{8,10},{9,13},{10,... | collective-permute-start | bytes 3145736 | tf_op jit(solution)/shard_map/ppermute | solution.py:520
  60.7 41.9 %copy-start.7 = (s32[20,2]{0,1:T(2,128)S(1)}, s32[20,2]{0,1:T(2,128)}, u32[]{:S(2)}) copy-start(s32[20,2]{0,1:T(2,128)} %param.9) | copy-start | bytes 484
  60.7 14.0 %collective-permute-start.6 = (f32[1,256,512]{2,1,0:T(8,128)S(1)}, f32[1,256,512]{2,1,0:T(8,128)S(1)}, u32[]{:S(2)}, u32[]{:S(2)}) collective-permute-start(f32[1,256,512]{2,1,0:T(8,128)S(1)} %fusion.1.refs_2_), channel_id=1, source_target_pairs={{8,0},{16,8},{24,16},{9,1},{17,9},{25,17},{10,2},{18,10},{26,18},{... | collective-permute-start | bytes 1572872 | tf_op jit(solution)/shard_map/ppermute | solution.py:536
  62.0 13.9 %collective-permute-start.3 = (f32[1,256,512]{2,1,0:T(8,128)S(1)}, f32[1,256,512]{2,1,0:T(8,128)S(1)}, u32[]{:S(2)}, u32[]{:S(2)}) collective-permute-start(f32[1,256,512]{2,1,0:T(8,128)S(1)} %fusion.1.refs_2_), channel_id=1, source_target_pairs={{0,8},{8,16},{16,24},{1,9},{9,17},{17,25},{2,10},{10,18},{18,26},{... | collective-permute-start | bytes 1572872 | tf_op jit(solution)/shard_map/ppermute | solution.py:532
  75.9 9.2 %collective-permute-start.7 = (f32[1,256,512]{2,1,0:T(8,128)S(1)}, f32[1,256,512]{2,1,0:T(8,128)S(1)}, u32[]{:S(2)}, u32[]{:S(2)}) collective-permute-start(f32[1,256,512]{2,1,0:T(8,128)S(1)} %slice_add_fusion.2), channel_id=1, source_target_pairs={{0,4},{1,3},{2,6},{3,1},{4,0},{5,7},{6,2},{7,5},{8,12},{9,11},{10,... | collective-permute-start | bytes 1572872 | tf_op jit(solution)/shard_map/ppermute | solution.py:520
  77.4 13.6 %collective-permute-start.10 = (f32[1,256,512]{2,1,0:T(8,128)S(1)}, f32[1,256,512]{2,1,0:T(8,128)S(1)}, u32[]{:S(2)}, u32[]{:S(2)}) collective-permute-start(f32[1,256,512]{2,1,0:T(8,128)S(1)} %collective-permute-done.6.refs_4_), channel_id=1, source_target_pairs={{8,0},{16,8},{24,16},{9,1},{17,9},{25,17},{10,2},{18,10},{26,18},{... | collective-permute-start | bytes 1572872 | tf_op jit(solution)/shard_map/ppermute | solution.py:536
  85.3 12.1 %collective-permute-start.8 = (f32[1,256,512]{2,1,0:T(8,128)S(1)}, f32[1,256,512]{2,1,0:T(8,128)S(1)}, u32[]{:S(2)}, u32[]{:S(2)}) collective-permute-start(f32[1,256,512]{2,1,0:T(8,128)S(1)} %fusion.refs_3_.refs_0_), channel_id=1, source_target_pairs={{0,8},{8,16},{16,24},{1,9},{9,17},{17,25},{2,10},{10,18},{18,26},{... | collective-permute-start | bytes 1572872 | tf_op jit(solution)/shard_map/ppermute | solution.py:532
  89.7 13.0 %collective-permute-start.9 = (f32[1,256,512]{2,1,0:T(8,128)S(1)}, f32[1,256,512]{2,1,0:T(8,128)S(1)}, u32[]{:S(2)}, u32[]{:S(2)}) collective-permute-start(f32[1,256,512]{2,1,0:T(8,128)S(1)} %fusion.refs_3_.refs_0_), channel_id=1, source_target_pairs={{8,0},{16,8},{24,16},{9,1},{17,9},{25,17},{10,2},{18,10},{26,18},{... | collective-permute-start | bytes 1572872 | tf_op jit(solution)/shard_map/ppermute | solution.py:536
  91.0 0.8 copy-start.2
  97.4 11.5 %collective-permute-start.11 = (f32[1,256,512]{2,1,0:T(8,128)S(1)}, f32[1,256,512]{2,1,0:T(8,128)}, u32[]{:S(2)}, u32[]{:S(2)}) collective-permute-start(f32[1,256,512]{2,1,0:T(8,128)S(1)} %collective-permute-done.8.refs_1_), channel_id=1, source_target_pairs={{0,8},{8,16},{16,24},{1,9},{9,17},{17,25},{2,10},{10,18},{18,26},{... | collective-permute-start | bytes 1572872 | tf_op jit(solution)/shard_map/ppermute | solution.py:532
  102.7 6.2 %copy-start.3 = (f32[1,256,512]{2,1,0:T(8,128)S(1)}, f32[1,256,512]{2,1,0:T(8,128)}, u32[]{:S(2)}) copy-start(f32[1,256,512]{2,1,0:T(8,128)} %copy-done.2) | copy-start | bytes 1572868
